TPU v7x, 256 devices: a whole 4x4x8 slice. The times are simulated.
256 devices in a mesh: cond: 4 (over z_hi), space: 64 (over z_lo, y, x, core).
Axes of the slice: x: 4, y: 4, z: 8 (z_hi: 4, z_lo: 2; z = z_hi * 2 + z_lo), core: 2. Of those that a mesh axis runs over, the one named last changes fastest.
Arguments:
- objective_grad: float32 [8, 5, 256, 8, 128], P('cond', None, 'space'), may hold values from -18 to 18
- shape_derivative: float32 [8, 5, 256, 8, 128], P('cond', None, 'space'), may hold values from -6 to 6
- flux_jacobian: float32 [8, 3, 5, 5], P('cond'), may hold values from -2 to 2
- sensor: float32 [8, 256, 8, 128], P('cond', 'space'), may hold values from 0.1 to 1
- pseudo_shift: float32 [8], P('cond'), may hold values from 1 to 3
- objective_weight: float32 [8], P('cond'), may hold values from 0.3 to 3
- agglomeration: int32 [256, 8, 128], P('space'), may hold values from 0 to 127, as said below
- coarse_links: int32 [6, 8192], P(None, 'space'), may hold values from 0 to 8191, as said below
Outputs:
- adjoint: float32 [8, 5, 256, 8, 128], P('cond', None, 'space')
- mesh_sensitivity: float32 [256, 8, 128], P('space', 'cond')
Inputs may be any that keep to these rules, and one draw needn't show every extreme that they name: `agglomeration`: each value names the cells of one box of 2 x 4 x 4 cells of the block (boxes aligned to the block), numbered in a random order within each block of 4 cells along the first dimension. `coarse_links`: the entries of a coarse cell are its six face neighbours on the grid of boxes; where a neighbour would lie outside the grid, the cell names itself. Every entry lies in the cell's own block or in a block beside it along the first dimension.
All inputs are finite; a program needn't handle non-finite values.
Results may differ from a plain program's by a relative error of at most 0.0001.
Values sent between devices are 32-bit elements; how exact they have to be, the bound alone decides.
A program may use at most 64 MiB of HBM per device.

v0:
```python
import jax
import jax.numpy as jnp
from jax import lax
from jax.sharding import PartitionSpec as P

AGG = 32
LINKS = 6
CYCLES = 2
SWEEPS = 3
CSWEEPS = 4


EPS_FOURTH = 1.0 / 32.0
RELAX = 0.7


def with_halo(cells, sides, width):
    for axis, dim in sides:
        count = lax.axis_size(axis)
        ends = count - 1
        head = lax.slice_in_dim(cells, 0, width, axis=dim)
        tail = lax.slice_in_dim(cells, cells.shape[dim] - width, cells.shape[dim], axis=dim)
        cells = jnp.concatenate(
            [
                lax.ppermute(tail, axis, [(i, (i + 1) % count) for i in range(ends)]),
                cells,
                lax.ppermute(head, axis, [((i + 1) % count, i) for i in range(ends)]),
            ],
            axis=dim,
        )
    return cells


def window(values, leading, margin, direction, displace):
    selection = []
    for i in range(values.ndim):
        if i < leading:
            selection.append(slice(None))
        else:
            length = values.shape[i] - 2 * margin
            offset = margin + (displace if i - leading == direction else 0)
            selection.append(slice(offset, offset + length))
    return values[tuple(selection)]


def coefficients(sensor_pad, shift):
    center = window(sensor_pad, 1, 1, 0, 0)
    face_plus = []
    face_minus = []
    summed = jnp.zeros_like(center)
    for d in range(3):
        face_plus.append((center + window(sensor_pad, 1, 1, d, 1)) * 0.25)
        face_minus.append((center + window(sensor_pad, 1, 1, d, -1)) * 0.25)
        summed = summed + (face_plus[d] + face_minus[d])
    diagonal_fine = shift[:, None, None, None] + summed + 18.0 * EPS_FOURTH
    return (face_plus, face_minus, diagonal_fine)


def operate(field_x, face_plus, face_minus, jacobians, shift):
    extended = jnp.pad(field_x, ((0, 0), (0, 0), (0, 0), (2, 2), (2, 2)))
    center = window(extended, 2, 2, 0, 0)
    result = shift[:, None, None, None, None] * center
    for d in range(3):
        plus_one = window(extended, 2, 2, d, 1)
        minus_one = window(extended, 2, 2, d, -1)
        plus_two = window(extended, 2, 2, d, 2)
        minus_two = window(extended, 2, 2, d, -2)
        central = 0.5 * jnp.einsum(
            "cuv,cuxyz->cvxyz",
            jacobians[:, d],
            minus_one - plus_one,
            precision=lax.Precision.HIGHEST,
        )
        second = face_plus[d][:, None] * (plus_one - center) - face_minus[d][:, None] * (
            center - minus_one
        )
        fourth = EPS_FOURTH * (plus_two + minus_two - 4.0 * (plus_one + minus_one) + 6.0 * center)
        result = result + (central - second + fourth)
    return result


def coarse_sweep(current, lookup, coarse_res, links, diagonal_coarse, coupling):
    neighbour_sum = jnp.sum(lookup[:, :, links], axis=2)
    return (
        current
        + (coarse_res - diagonal_coarse * current + coupling * neighbour_sum) / diagonal_coarse
    )


def local(
    objective_grad,
    shape_derivative,
    flux_jacobian,
    sensor,
    pseudo_shift,
    objective_weight,
    agglomeration,
    coarse_links,
):
    local_ids = agglomeration.reshape(-1)
    coupling = AGG / 4.0
    conditions = objective_grad.shape[0]
    coarse_count = coarse_links.shape[1]
    block = lax.axis_index("space")
    near_links = coarse_links - (block - 1) * coarse_count
    diagonal_coarse = (pseudo_shift * AGG + LINKS * AGG / 4.0)[:, None, None]
    adjoint = jnp.zeros_like(objective_grad)
    sensor_rim = with_halo(sensor, (("space", 1),), 1)
    sensor_pad = jnp.pad(sensor_rim, ((0, 0), (0, 0), (1, 1), (1, 1)))
    face_plus, face_minus, diagonal_fine = coefficients(sensor_pad, pseudo_shift)

    def residual_of(adjoint):
        padded = with_halo(adjoint, (("space", 2),), 2)
        return objective_grad - operate(padded, face_plus, face_minus, flux_jacobian, pseudo_shift)

    for cycle in range(CYCLES):
        for sweep in range(SWEEPS):
            adjoint = adjoint + RELAX * residual_of(adjoint) / diagonal_fine[:, None]
        fine_res = residual_of(adjoint)
        flattened = fine_res.reshape(conditions * 5, -1)
        restrict_coarse_res = jax.ops.segment_sum(
            flattened.T, local_ids, num_segments=coarse_count
        ).T.reshape(conditions, 5, coarse_count)
        correction = restrict_coarse_res / diagonal_coarse
        for step in range(CSWEEPS - 1):
            lookup = with_halo(correction, (("space", 2),), coarse_count)
            correction = coarse_sweep(
                correction, lookup, restrict_coarse_res, near_links, diagonal_coarse, coupling
            )
        adjoint = adjoint + correction[:, :, local_ids].reshape(adjoint.shape)
    per_condition = objective_weight[:, None, None, None] * jnp.sum(
        adjoint * shape_derivative, axis=1
    )
    contribution = jnp.sum(per_condition, axis=0)
    mesh_sensitivity = lax.psum_scatter(contribution, "cond", scatter_dimension=1, tiled=True)
    return (adjoint, mesh_sensitivity)


def solution(mesh):
    in_specs = (
        P("cond", None, "space", None, None),
        P("cond", None, "space", None, None),
        P("cond", None, None, None),
        P("cond", "space", None, None),
        P("cond"),
        P("cond"),
        P("space", None, None),
        P(None, "space"),
    )
    out_specs = (P("cond", None, "space", None, None), P("space", "cond", None))
    return jax.shard_map(local, mesh=mesh, in_specs=in_specs, out_specs=out_specs, check_vma=False)
```

profile of v0, /device:TPU:32, one launch (start us, length us, event | category | flops | bytes accessed | tf_op | source)
XLA Modules:
  0.0 358.7 jit_solution(876593605194091169)
XLA Ops:
  0.6 1.9 collective-permute-start
  2.6 7.9 %collective-permute-start.1 = (f32[2,5,2,8,128]{4,1,3,2,0:T(8,128)S(1)}, f32[2,5,2,8,128]{4,1,3,2,0:T(8,128)S(1)}, u32[]{:S(2)}, u32[]{:S(2)}) collective-permute-start(f32[2,5,2,8,128]{4,1,3,2,0:T(8,128)S(1)} %broadcast.122), channel_id=1, source_target_pairs={{1,0},{2,1},{3,2},{4,3},{5,4},{6,5},{7,6},{8,7},{9,8},{10,9},{11,1... | collective-permute-start | bytes 245768 | tf_op jit(solution)/shard_map/ppermute | solution.py:27
  11.2 1.9 collective-permute-start.2
  13.1 2.4 collective-permute-start.3
  17.2 5.1 %collective-permute-done.3 = f32[2,1,8,128]{3,2,1,0:T(8,128)S(1)} collective-permute-done((f32[2,1,8,128]{3,2,1,0:T(8,128)S(1)}, f32[2,1,8,128]{3,2,1,0:T(8,128)S(1)}, u32[]{:S(2)}, u32[]{:S(2)}) %collective-permute-start.3) | collective-permute-done | bytes 8224 | tf_op jit(solution)/shard_map/ppermute | solution.py:25
  26.3 1.9 collective-permute-start.4
  28.2 7.9 %collective-permute-start.5 = (f32[2,5,2,8,128]{4,1,3,2,0:T(8,128)S(1)}, f32[2,5,2,8,128]{4,1,3,2,0:T(8,128)S(1)}, u32[]{:S(2)}, u32[]{:S(2)}) collective-permute-start(f32[2,5,2,8,128]{4,1,3,2,0:T(8,128)S(1)} %get-tuple-element.36), channel_id=1, source_target_pairs={{1,0},{2,1},{3,2},{4,3},{5,4},{6,5},{7,6},{8,7},{9,8},{10,9},{11,1... | collective-permute-start | bytes 245768 | tf_op jit(solution)/shard_map/ppermute | solution.py:27
  36.8 1.8 collective-permute-done.5
  41.0 1.9 collective-permute-start.6
  42.9 8.0 %collective-permute-start.7 = (f32[2,5,2,8,128]{4,1,3,2,0:T(8,128)S(1)}, f32[2,5,2,8,128]{4,1,3,2,0:T(8,128)S(1)}, u32[]{:S(2)}, u32[]{:S(2)}) collective-permute-start(f32[2,5,2,8,128]{4,1,3,2,0:T(8,128)S(1)} %get-tuple-element.34), channel_id=1, source_target_pairs={{1,0},{2,1},{3,2},{4,3},{5,4},{6,5},{7,6},{8,7},{9,8},{10,9},{11,1... | collective-permute-start | bytes 245768 | tf_op jit(solution)/shard_map/ppermute | solution.py:27
  55.7 1.9 collective-permute-start.8
  57.6 8.0 %collective-permute-start.9 = (f32[2,5,2,8,128]{4,1,3,2,0:T(8,128)S(1)}, f32[2,5,2,8,128]{4,1,3,2,0:T(8,128)S(1)}, u32[]{:S(2)}, u32[]{:S(2)}) collective-permute-start(f32[2,5,2,8,128]{4,1,3,2,0:T(8,128)S(1)} %get-tuple-element.32), channel_id=1, source_target_pairs={{1,0},{2,1},{3,2},{4,3},{5,4},{6,5},{7,6},{8,7},{9,8},{10,9},{11,1... | collective-permute-start | bytes 245768 | tf_op jit(solution)/shard_map/ppermute | solution.py:27
  71.0 24.0 %scatter_custom_fusion = f32[128,10]{1,0:T(8,128)S(1)} fusion(s32[4096]{0:T(1024)S(1)} %bitcast.356, f32[4096,10]{1,0:T(8,128)S(1)} %copy.330, f32[]{:T(128)} %constant.16.clone.1), kind=kCustom, calls=%fused_computation.413 | custom fusion | flops 40960 | bytes 5124 | tf_op jit(solution)/shard_map/scatter-add | solution.py:121
  95.2 1.9 collective-permute-start.10
  97.1 8.2 %collective-permute-start.11 = (f32[2,5,128]{2,0,1:T(2,128)S(1)}, f32[2,5,128]{2,0,1:T(2,128)S(1)}, u32[]{:S(2)}, u32[]{:S(2)}) collective-permute-start(f32[2,5,128]{2,0,1:T(2,128)S(1)} %broadcast_divide_fusion.1), channel_id=1, source_target_pairs={{1,0},{2,1},{3,2},{4,3},{5,4},{6,5},{7,6},{8,7},{9,8},{10,9},{11,1... | collective-permute-start | bytes 15368 | tf_op jit(solution)/shard_map/ppermute | solution.py:27
  106.7 2.8 gather_fusion
  110.2 1.9 collective-permute-start.12
  112.1 7.9 %collective-permute-start.13 = (f32[2,5,128]{2,0,1:T(2,128)S(1)}, f32[2,5,128]{2,0,1:T(2,128)S(1)}, u32[]{:S(2)}, u32[]{:S(2)}) collective-permute-start(f32[2,5,128]{2,0,1:T(2,128)S(1)} %divide_add_fusion.5), channel_id=1, source_target_pairs={{1,0},{2,1},{3,2},{4,3},{5,4},{6,5},{7,6},{8,7},{9,8},{10,9},{11,1... | collective-permute-start | bytes 15368 | tf_op jit(solution)/shard_map/ppermute | solution.py:27
  121.5 2.8 gather_fusion.1
  125.0 1.9 collective-permute-start.14
  127.0 7.9 %collective-permute-start.15 = (f32[2,5,128]{2,0,1:T(2,128)S(1)}, f32[2,5,128]{2,0,1:T(2,128)S(1)}, u32[]{:S(2)}, u32[]{:S(2)}) collective-permute-start(f32[2,5,128]{2,0,1:T(2,128)S(1)} %divide_add_fusion.4), channel_id=1, source_target_pairs={{1,0},{2,1},{3,2},{4,3},{5,4},{6,5},{7,6},{8,7},{9,8},{10,9},{11,1... | collective-permute-start | bytes 15368 | tf_op jit(solution)/shard_map/ppermute | solution.py:27
  136.4 2.8 gather_fusion.2
  140.0 28.5 %gather_fusion.3 = f32[4096,2,5]{2,1,0:T(2,128)} fusion(f32[2,5,128]{1,0,2:T(2,128)S(1)} %copy.342, s32[4096]{0:T(1024)S(1)} %broadcast_clamp_fusion), kind=kCustom, calls=%fused_computation.3 | custom fusion | bytes 344064 | tf_op jit(solution)/shard_map/gather | solution.py:130
  168.6 5.2 %copy.344 = f32[2,5,4,8,128]{4,1,3,2,0:T(8,128)S(1)} copy(f32[2,5,4,8,128]{1,0,4,3,2:T(2,128)} %bitcast.344) | data formatting | bytes 327680 | tf_op jit(solution)/shard_map/reshape | solution.py:130
  173.9 1.9 collective-permute-start.16
  175.8 7.9 %collective-permute-start.17 = (f32[2,5,2,8,128]{4,1,3,2,0:T(8,128)S(1)}, f32[2,5,2,8,128]{4,1,3,2,0:T(8,128)S(1)}, u32[]{:S(2)}, u32[]{:S(2)}) collective-permute-start(f32[2,5,2,8,128]{4,1,3,2,0:T(8,128)S(1)} %get-tuple-element.30), channel_id=1, source_target_pairs={{1,0},{2,1},{3,2},{4,3},{5,4},{6,5},{7,6},{8,7},{9,8},{10,9},{11,1... | collective-permute-start | bytes 245768 | tf_op jit(solution)/shard_map/ppermute | solution.py:27
  184.4 1.8 collective-permute-done.17
  188.4 1.9 collective-permute-start.18
  190.3 8.0 %collective-permute-start.19 = (f32[2,5,2,8,128]{4,1,3,2,0:T(8,128)S(1)}, f32[2,5,2,8,128]{4,1,3,2,0:T(8,128)S(1)}, u32[]{:S(2)}, u32[]{:S(2)}) collective-permute-start(f32[2,5,2,8,128]{4,1,3,2,0:T(8,128)S(1)} %get-tuple-element.28), channel_id=1, source_target_pairs={{1,0},{2,1},{3,2},{4,3},{5,4},{6,5},{7,6},{8,7},{9,8},{10,9},{11,1... | collective-permute-start | bytes 245768 | tf_op jit(solution)/shard_map/ppermute | solution.py:27
  203.0 1.9 collective-permute-start.20
  205.0 8.0 %collective-permute-start.21 = (f32[2,5,2,8,128]{4,1,3,2,0:T(8,128)S(1)}, f32[2,5,2,8,128]{4,1,3,2,0:T(8,128)S(1)}, u32[]{:S(2)}, u32[]{:S(2)}) collective-permute-start(f32[2,5,2,8,128]{4,1,3,2,0:T(8,128)S(1)} %get-tuple-element.26), channel_id=1, source_target_pairs={{1,0},{2,1},{3,2},{4,3},{5,4},{6,5},{7,6},{8,7},{9,8},{10,9},{11,1... | collective-permute-start | bytes 245768 | tf_op jit(solution)/shard_map/ppermute | solution.py:27
  213.7 1.8 collective-permute-done.21
  217.7 1.9 collective-permute-start.22
  219.6 8.2 %collective-permute-start.23 = (f32[2,5,2,8,128]{4,1,3,2,0:T(8,128)S(1)}, f32[2,5,2,8,128]{4,1,3,2,0:T(8,128)S(1)}, u32[]{:S(2)}, u32[]{:S(2)}) collective-permute-start(f32[2,5,2,8,128]{4,1,3,2,0:T(8,128)S(1)} %get-tuple-element.24), channel_id=1, source_target_pairs={{1,0},{2,1},{3,2},{4,3},{5,4},{6,5},{7,6},{8,7},{9,8},{10,9},{11,1... | collective-permute-start | bytes 245768 | tf_op jit(solution)/shard_map/ppermute | solution.py:27
  228.3 1.8 collective-permute-done.23
  233.0 24.0 %scatter_custom_fusion.1 = f32[128,10]{1,0:T(8,128)S(1)} fusion(s32[4096]{0:T(1024)S(1)} %bitcast.358, f32[4096,10]{1,0:T(8,128)S(1)} %copy.362, f32[]{:T(128)} %constant.16.clone.1), kind=kCustom, calls=%fused_computation.411 | custom fusion | flops 40960 | bytes 5124 | tf_op jit(solution)/shard_map/scatter-add | solution.py:121
  257.2 1.9 collective-permute-start.24
  259.1 8.0 %collective-permute-start.25 = (f32[2,5,128]{2,0,1:T(2,128)S(1)}, f32[2,5,128]{2,0,1:T(2,128)S(1)}, u32[]{:S(2)}, u32[]{:S(2)}) collective-permute-start(f32[2,5,128]{2,0,1:T(2,128)S(1)} %broadcast_divide_fusion), channel_id=1, source_target_pairs={{1,0},{2,1},{3,2},{4,3},{5,4},{6,5},{7,6},{8,7},{9,8},{10,9},{11,1... | collective-permute-start | bytes 15368 | tf_op jit(solution)/shard_map/ppermute | solution.py:27
  268.7 2.8 gather_fusion.4
  272.2 1.9 collective-permute-start.26
  274.1 7.9 %collective-permute-start.27 = (f32[2,5,128]{2,0,1:T(2,128)S(1)}, f32[2,5,128]{2,0,1:T(2,128)S(1)}, u32[]{:S(2)}, u32[]{:S(2)}) collective-permute-start(f32[2,5,128]{2,0,1:T(2,128)S(1)} %divide_add_fusion.2), channel_id=1, source_target_pairs={{1,0},{2,1},{3,2},{4,3},{5,4},{6,5},{7,6},{8,7},{9,8},{10,9},{11,1... | collective-permute-start | bytes 15368 | tf_op jit(solution)/shard_map/ppermute | solution.py:27
  283.5 2.8 gather_fusion.5
  287.0 1.9 collective-permute-start.28
  288.9 7.9 %collective-permute-start.29 = (f32[2,5,128]{2,0,1:T(2,128)S(1)}, f32[2,5,128]{2,0,1:T(2,128)S(1)}, u32[]{:S(2)}, u32[]{:S(2)}) collective-permute-start(f32[2,5,128]{2,0,1:T(2,128)S(1)} %divide_add_fusion.1), channel_id=1, source_target_pairs={{1,0},{2,1},{3,2},{4,3},{5,4},{6,5},{7,6},{8,7},{9,8},{10,9},{11,1... | collective-permute-start | bytes 15368 | tf_op jit(solution)/shard_map/ppermute | solution.py:27
  298.3 2.8 gather_fusion.6
  302.0 28.5 %gather_fusion.7 = f32[4096,2,5]{2,1,0:T(2,128)} fusion(f32[2,5,128]{1,0,2:T(2,128)S(1)} %copy.374, s32[4096]{0:T(1024)S(1)} %broadcast_clamp_fusion), kind=kCustom, calls=%fused_computation.7 | custom fusion | bytes 344064 | tf_op jit(solution)/shard_map/gather | solution.py:130
  330.5 5.3 %copy.376 = f32[2,5,4,8,128]{4,1,3,2,0:T(8,128)S(1)} copy(f32[2,5,4,8,128]{1,0,4,3,2:T(2,128)} %bitcast.343) | data formatting | bytes 327680 | tf_op jit(solution)/shard_map/reshape | solution.py:130
  336.8 21.3 %all-reduce.11 = f32[4,8,128]{2,0,1:T(4,128)S(1)} all-reduce(f32[4,8,128]{2,0,1:T(4,128)S(1)} %copy.378), channel_id=2, replica_groups=mesh['cond'=4,'space'=64] {'cond'}, use_global_device_ids=true, to_apply=%region_10.11.clone | all-reduce | flops 4096 | bytes 32768
  (144 shorter events, 47.6 us)
Async XLA Ops:
  0.6 23.5 %collective-permute-start = (f32[2,5,2,8,128]{4,1,3,2,0:T(8,128)S(1)}, f32[2,5,2,8,128]{4,1,3,2,0:T(8,128)S(1)}, u32[]{:S(2)}, u32[]{:S(2)}) collective-permute-start(f32[2,5,2,8,128]{4,1,3,2,0:T(8,128)S(1)} %broadcast.122), channel_id=1, source_target_pairs={{0,1},{1,2},{2,3},{3,4},{4,5},{5,6},{6,7},{7,8},{8,9},{9,10},{10,1... | collective-permute-start | bytes 245768 | tf_op jit(solution)/shard_map/ppermute | solution.py:25
  2.6 21.6 %collective-permute-start.1 = (f32[2,5,2,8,128]{4,1,3,2,0:T(8,128)S(1)}, f32[2,5,2,8,128]{4,1,3,2,0:T(8,128)S(1)}, u32[]{:S(2)}, u32[]{:S(2)}) collective-permute-start(f32[2,5,2,8,128]{4,1,3,2,0:T(8,128)S(1)} %broadcast.122), channel_id=1, source_target_pairs={{1,0},{2,1},{3,2},{4,3},{5,4},{6,5},{7,6},{8,7},{9,8},{10,9},{11,1... | collective-permute-start | bytes 245768 | tf_op jit(solution)/shard_map/ppermute | solution.py:27
  11.2 6.0 %collective-permute-start.2 = (f32[2,1,8,128]{3,2,1,0:T(8,128)S(1)}, f32[2,1,8,128]{3,2,1,0:T(8,128)S(1)}, u32[]{:S(2)}, u32[]{:S(2)}) collective-permute-start(f32[2,1,8,128]{3,2,1,0:T(8,128)S(1)} %get-tuple-element.37), channel_id=1, source_target_pairs={{1,0},{2,1},{3,2},{4,3},{5,4},{6,5},{7,6},{8,7},{9,8},{10,9},{11,1... | collective-permute-start | bytes 24584 | tf_op jit(solution)/shard_map/ppermute | solution.py:27
  13.1 9.2 %collective-permute-start.3 = (f32[2,1,8,128]{3,2,1,0:T(8,128)S(1)}, f32[2,1,8,128]{3,2,1,0:T(8,128)S(1)}, u32[]{:S(2)}, u32[]{:S(2)}) collective-permute-start(f32[2,1,8,128]{3,2,1,0:T(8,128)S(1)} %get-tuple-element.38), channel_id=1, source_target_pairs={{0,1},{1,2},{2,3},{3,4},{4,5},{5,6},{6,7},{7,8},{8,9},{9,10},{10,1... | collective-permute-start | bytes 24584 | tf_op jit(solution)/shard_map/ppermute | solution.py:25
  24.5 1.2 copy-start.5
  26.3 10.5 %collective-permute-start.4 = (f32[2,5,2,8,128]{4,1,3,2,0:T(8,128)S(1)}, f32[2,5,2,8,128]{4,1,3,2,0:T(8,128)S(1)}, u32[]{:S(2)}, u32[]{:S(2)}) collective-permute-start(f32[2,5,2,8,128]{4,1,3,2,0:T(8,128)S(1)} %get-tuple-element.35), channel_id=1, source_target_pairs={{0,1},{1,2},{2,3},{3,4},{4,5},{5,6},{6,7},{7,8},{8,9},{9,10},{10,1... | collective-permute-start | bytes 245768 | tf_op jit(solution)/shard_map/ppermute | solution.py:25
  28.2 10.4 %collective-permute-start.5 = (f32[2,5,2,8,128]{4,1,3,2,0:T(8,128)S(1)}, f32[2,5,2,8,128]{4,1,3,2,0:T(8,128)S(1)}, u32[]{:S(2)}, u32[]{:S(2)}) collective-permute-start(f32[2,5,2,8,128]{4,1,3,2,0:T(8,128)S(1)} %get-tuple-element.36), channel_id=1, source_target_pairs={{1,0},{2,1},{3,2},{4,3},{5,4},{6,5},{7,6},{8,7},{9,8},{10,9},{11,1... | collective-permute-start | bytes 245768 | tf_op jit(solution)/shard_map/ppermute | solution.py:27
  39.5 0.7 copy-start.3
  41.0 10.6 %collective-permute-start.6 = (f32[2,5,2,8,128]{4,1,3,2,0:T(8,128)S(1)}, f32[2,5,2,8,128]{4,1,3,2,0:T(8,128)S(1)}, u32[]{:S(2)}, u32[]{:S(2)}) collective-permute-start(f32[2,5,2,8,128]{4,1,3,2,0:T(8,128)S(1)} %get-tuple-element.33), channel_id=1, source_target_pairs={{0,1},{1,2},{2,3},{3,4},{4,5},{5,6},{6,7},{7,8},{8,9},{9,10},{10,1... | collective-permute-start | bytes 245768 | tf_op jit(solution)/shard_map/ppermute | solution.py:25
  42.9 10.5 %collective-permute-start.7 = (f32[2,5,2,8,128]{4,1,3,2,0:T(8,128)S(1)}, f32[2,5,2,8,128]{4,1,3,2,0:T(8,128)S(1)}, u32[]{:S(2)}, u32[]{:S(2)}) collective-permute-start(f32[2,5,2,8,128]{4,1,3,2,0:T(8,128)S(1)} %get-tuple-element.34), channel_id=1, source_target_pairs={{1,0},{2,1},{3,2},{4,3},{5,4},{6,5},{7,6},{8,7},{9,8},{10,9},{11,1... | collective-permute-start | bytes 245768 | tf_op jit(solution)/shard_map/ppermute | solution.py:27
  54.9 10.8 %copy-start.2 = (s32[6,128]{1,0:T(8,128)S(1)}, s32[6,128]{1,0:T(8,128)}, u32[]{:S(2)}) copy-start(s32[6,128]{1,0:T(8,128)} %param.15) | copy-start | bytes 9220
  55.7 10.6 %collective-permute-start.8 = (f32[2,5,2,8,128]{4,1,3,2,0:T(8,128)S(1)}, f32[2,5,2,8,128]{4,1,3,2,0:T(8,128)S(1)}, u32[]{:S(2)}, u32[]{:S(2)}) collective-permute-start(f32[2,5,2,8,128]{4,1,3,2,0:T(8,128)S(1)} %get-tuple-element.31), channel_id=1, source_target_pairs={{0,1},{1,2},{2,3},{3,4},{4,5},{5,6},{6,7},{7,8},{8,9},{9,10},{10,1... | collective-permute-start | bytes 245768 | tf_op jit(solution)/shard_map/ppermute | solution.py:25
  57.6 10.5 %collective-permute-start.9 = (f32[2,5,2,8,128]{4,1,3,2,0:T(8,128)S(1)}, f32[2,5,2,8,128]{4,1,3,2,0:T(8,128)S(1)}, u32[]{:S(2)}, u32[]{:S(2)}) collective-permute-start(f32[2,5,2,8,128]{4,1,3,2,0:T(8,128)S(1)} %get-tuple-element.32), channel_id=1, source_target_pairs={{1,0},{2,1},{3,2},{4,3},{5,4},{6,5},{7,6},{8,7},{9,8},{10,9},{11,1... | collective-permute-start | bytes 245768 | tf_op jit(solution)/shard_map/ppermute | solution.py:27
  70.3 0.7 copy-start.1
  95.2 10.1 %collective-permute-start.10 = (f32[2,5,128]{2,0,1:T(2,128)S(1)}, f32[2,5,128]{2,0,1:T(2,128)S(1)}, u32[]{:S(2)}, u32[]{:S(2)}) collective-permute-start(f32[2,5,128]{2,0,1:T(2,128)S(1)} %broadcast_divide_fusion.1), channel_id=1, source_target_pairs={{0,1},{1,2},{2,3},{3,4},{4,5},{5,6},{6,7},{7,8},{8,9},{9,10},{10,1... | collective-permute-start | bytes 15368 | tf_op jit(solution)/shard_map/ppermute | solution.py:25
  97.1 9.3 %collective-permute-start.11 = (f32[2,5,128]{2,0,1:T(2,128)S(1)}, f32[2,5,128]{2,0,1:T(2,128)S(1)}, u32[]{:S(2)}, u32[]{:S(2)}) collective-permute-start(f32[2,5,128]{2,0,1:T(2,128)S(1)} %broadcast_divide_fusion.1), channel_id=1, source_target_pairs={{1,0},{2,1},{3,2},{4,3},{5,4},{6,5},{7,6},{8,7},{9,8},{10,9},{11,1... | collective-permute-start | bytes 15368 | tf_op jit(solution)/shard_map/ppermute | solution.py:27
  110.2 9.8 %collective-permute-start.12 = (f32[2,5,128]{2,0,1:T(2,128)S(1)}, f32[2,5,128]{2,0,1:T(2,128)S(1)}, u32[]{:S(2)}, u32[]{:S(2)}) collective-permute-start(f32[2,5,128]{2,0,1:T(2,128)S(1)} %divide_add_fusion.5), channel_id=1, source_target_pairs={{0,1},{1,2},{2,3},{3,4},{4,5},{5,6},{6,7},{7,8},{8,9},{9,10},{10,1... | collective-permute-start | bytes 15368 | tf_op jit(solution)/shard_map/ppermute | solution.py:25
  112.1 9.2 %collective-permute-start.13 = (f32[2,5,128]{2,0,1:T(2,128)S(1)}, f32[2,5,128]{2,0,1:T(2,128)S(1)}, u32[]{:S(2)}, u32[]{:S(2)}) collective-permute-start(f32[2,5,128]{2,0,1:T(2,128)S(1)} %divide_add_fusion.5), channel_id=1, source_target_pairs={{1,0},{2,1},{3,2},{4,3},{5,4},{6,5},{7,6},{8,7},{9,8},{10,9},{11,1... | collective-permute-start | bytes 15368 | tf_op jit(solution)/shard_map/ppermute | solution.py:27
  125.0 9.8 %collective-permute-start.14 = (f32[2,5,128]{2,0,1:T(2,128)S(1)}, f32[2,5,128]{2,0,1:T(2,128)S(1)}, u32[]{:S(2)}, u32[]{:S(2)}) collective-permute-start(f32[2,5,128]{2,0,1:T(2,128)S(1)} %divide_add_fusion.4), channel_id=1, source_target_pairs={{0,1},{1,2},{2,3},{3,4},{4,5},{5,6},{6,7},{7,8},{8,9},{9,10},{10,1... | collective-permute-start | bytes 15368 | tf_op jit(solution)/shard_map/ppermute | solution.py:25
  127.0 9.2 %collective-permute-start.15 = (f32[2,5,128]{2,0,1:T(2,128)S(1)}, f32[2,5,128]{2,0,1:T(2,128)S(1)}, u32[]{:S(2)}, u32[]{:S(2)}) collective-permute-start(f32[2,5,128]{2,0,1:T(2,128)S(1)} %divide_add_fusion.4), channel_id=1, source_target_pairs={{1,0},{2,1},{3,2},{4,3},{5,4},{6,5},{7,6},{8,7},{9,8},{10,9},{11,1... | collective-permute-start | bytes 15368 | tf_op jit(solution)/shard_map/ppermute | solution.py:27
  173.9 10.5 %collective-permute-start.16 = (f32[2,5,2,8,128]{4,1,3,2,0:T(8,128)S(1)}, f32[2,5,2,8,128]{4,1,3,2,0:T(8,128)S(1)}, u32[]{:S(2)}, u32[]{:S(2)}) collective-permute-start(f32[2,5,2,8,128]{4,1,3,2,0:T(8,128)S(1)} %get-tuple-element.29), channel_id=1, source_target_pairs={{0,1},{1,2},{2,3},{3,4},{4,5},{5,6},{6,7},{7,8},{8,9},{9,10},{10,1... | collective-permute-start | bytes 245768 | tf_op jit(solution)/shard_map/ppermute | solution.py:25
  175.8 10.4 %collective-permute-start.17 = (f32[2,5,2,8,128]{4,1,3,2,0:T(8,128)S(1)}, f32[2,5,2,8,128]{4,1,3,2,0:T(8,128)S(1)}, u32[]{:S(2)}, u32[]{:S(2)}) collective-permute-start(f32[2,5,2,8,128]{4,1,3,2,0:T(8,128)S(1)} %get-tuple-element.30), channel_id=1, source_target_pairs={{1,0},{2,1},{3,2},{4,3},{5,4},{6,5},{7,6},{8,7},{9,8},{10,9},{11,1... | collective-permute-start | bytes 245768 | tf_op jit(solution)/shard_map/ppermute | solution.py:27
  188.4 10.6 %collective-permute-start.18 = (f32[2,5,2,8,128]{4,1,3,2,0:T(8,128)S(1)}, f32[2,5,2,8,128]{4,1,3,2,0:T(8,128)S(1)}, u32[]{:S(2)}, u32[]{:S(2)}) collective-permute-start(f32[2,5,2,8,128]{4,1,3,2,0:T(8,128)S(1)} %get-tuple-element.27), channel_id=1, source_target_pairs={{0,1},{1,2},{2,3},{3,4},{4,5},{5,6},{6,7},{7,8},{8,9},{9,10},{10,1... | collective-permute-start | bytes 245768 | tf_op jit(solution)/shard_map/ppermute | solution.py:25
  190.3 10.5 %collective-permute-start.19 = (f32[2,5,2,8,128]{4,1,3,2,0:T(8,128)S(1)}, f32[2,5,2,8,128]{4,1,3,2,0:T(8,128)S(1)}, u32[]{:S(2)}, u32[]{:S(2)}) collective-permute-start(f32[2,5,2,8,128]{4,1,3,2,0:T(8,128)S(1)} %get-tuple-element.28), channel_id=1, source_target_pairs={{1,0},{2,1},{3,2},{4,3},{5,4},{6,5},{7,6},{8,7},{9,8},{10,9},{11,1... | collective-permute-start | bytes 245768 | tf_op jit(solution)/shard_map/ppermute | solution.py:27
  203.0 10.6 %collective-permute-start.20 = (f32[2,5,2,8,128]{4,1,3,2,0:T(8,128)S(1)}, f32[2,5,2,8,128]{4,1,3,2,0:T(8,128)S(1)}, u32[]{:S(2)}, u32[]{:S(2)}) collective-permute-start(f32[2,5,2,8,128]{4,1,3,2,0:T(8,128)S(1)} %get-tuple-element.25), channel_id=1, source_target_pairs={{0,1},{1,2},{2,3},{3,4},{4,5},{5,6},{6,7},{7,8},{8,9},{9,10},{10,1... | collective-permute-start | bytes 245768 | tf_op jit(solution)/shard_map/ppermute | solution.py:25
  205.0 10.5 %collective-permute-start.21 = (f32[2,5,2,8,128]{4,1,3,2,0:T(8,128)S(1)}, f32[2,5,2,8,128]{4,1,3,2,0:T(8,128)S(1)}, u32[]{:S(2)}, u32[]{:S(2)}) collective-permute-start(f32[2,5,2,8,128]{4,1,3,2,0:T(8,128)S(1)} %get-tuple-element.26), channel_id=1, source_target_pairs={{1,0},{2,1},{3,2},{4,3},{5,4},{6,5},{7,6},{8,7},{9,8},{10,9},{11,1... | collective-permute-start | bytes 245768 | tf_op jit(solution)/shard_map/ppermute | solution.py:27
  217.7 10.6 %collective-permute-start.22 = (f32[2,5,2,8,128]{4,1,3,2,0:T(8,128)S(1)}, f32[2,5,2,8,128]{4,1,3,2,0:T(8,128)S(1)}, u32[]{:S(2)}, u32[]{:S(2)}) collective-permute-start(f32[2,5,2,8,128]{4,1,3,2,0:T(8,128)S(1)} %get-tuple-element.23), channel_id=1, source_target_pairs={{0,1},{1,2},{2,3},{3,4},{4,5},{5,6},{6,7},{7,8},{8,9},{9,10},{10,1... | collective-permute-start | bytes 245768 | tf_op jit(solution)/shard_map/ppermute | solution.py:25
  219.6 10.5 %collective-permute-start.23 = (f32[2,5,2,8,128]{4,1,3,2,0:T(8,128)S(1)}, f32[2,5,2,8,128]{4,1,3,2,0:T(8,128)S(1)}, u32[]{:S(2)}, u32[]{:S(2)}) collective-permute-start(f32[2,5,2,8,128]{4,1,3,2,0:T(8,128)S(1)} %get-tuple-element.24), channel_id=1, source_target_pairs={{1,0},{2,1},{3,2},{4,3},{5,4},{6,5},{7,6},{8,7},{9,8},{10,9},{11,1... | collective-permute-start | bytes 245768 | tf_op jit(solution)/shard_map/ppermute | solution.py:27
  257.2 10.0 %collective-permute-start.24 = (f32[2,5,128]{2,0,1:T(2,128)S(1)}, f32[2,5,128]{2,0,1:T(2,128)S(1)}, u32[]{:S(2)}, u32[]{:S(2)}) collective-permute-start(f32[2,5,128]{2,0,1:T(2,128)S(1)} %broadcast_divide_fusion), channel_id=1, source_target_pairs={{0,1},{1,2},{2,3},{3,4},{4,5},{5,6},{6,7},{7,8},{8,9},{9,10},{10,1... | collective-permute-start | bytes 15368 | tf_op jit(solution)/shard_map/ppermute | solution.py:25
  259.1 9.3 %collective-permute-start.25 = (f32[2,5,128]{2,0,1:T(2,128)S(1)}, f32[2,5,128]{2,0,1:T(2,128)S(1)}, u32[]{:S(2)}, u32[]{:S(2)}) collective-permute-start(f32[2,5,128]{2,0,1:T(2,128)S(1)} %broadcast_divide_fusion), channel_id=1, source_target_pairs={{1,0},{2,1},{3,2},{4,3},{5,4},{6,5},{7,6},{8,7},{9,8},{10,9},{11,1... | collective-permute-start | bytes 15368 | tf_op jit(solution)/shard_map/ppermute | solution.py:27
  268.4 28.4 %copy-start.6 = (u32[256]{0:T(256)S(1)}, u32[256]{0:T(256)}, u32[]{:S(2)}) copy-start(u32[256]{0:T(256)} %constant.74) | copy-start | bytes 3076
  272.2 9.8 %collective-permute-start.26 = (f32[2,5,128]{2,0,1:T(2,128)S(1)}, f32[2,5,128]{2,0,1:T(2,128)S(1)}, u32[]{:S(2)}, u32[]{:S(2)}) collective-permute-start(f32[2,5,128]{2,0,1:T(2,128)S(1)} %divide_add_fusion.2), channel_id=1, source_target_pairs={{0,1},{1,2},{2,3},{3,4},{4,5},{5,6},{6,7},{7,8},{8,9},{9,10},{10,1... | collective-permute-start | bytes 15368 | tf_op jit(solution)/shard_map/ppermute | solution.py:25
  274.1 9.2 %collective-permute-start.27 = (f32[2,5,128]{2,0,1:T(2,128)S(1)}, f32[2,5,128]{2,0,1:T(2,128)S(1)}, u32[]{:S(2)}, u32[]{:S(2)}) collective-permute-start(f32[2,5,128]{2,0,1:T(2,128)S(1)} %divide_add_fusion.2), channel_id=1, source_target_pairs={{1,0},{2,1},{3,2},{4,3},{5,4},{6,5},{7,6},{8,7},{9,8},{10,9},{11,1... | collective-permute-start | bytes 15368 | tf_op jit(solution)/shard_map/ppermute | solution.py:27
  287.0 11.1 %collective-permute-start.28 = (f32[2,5,128]{2,0,1:T(2,128)S(1)}, f32[2,5,128]{2,0,1:T(2,128)S(1)}, u32[]{:S(2)}, u32[]{:S(2)}) collective-permute-start(f32[2,5,128]{2,0,1:T(2,128)S(1)} %divide_add_fusion.1), channel_id=1, source_target_pairs={{0,1},{1,2},{2,3},{3,4},{4,5},{5,6},{6,7},{7,8},{8,9},{9,10},{10,1... | collective-permute-start | bytes 15368 | tf_op jit(solution)/shard_map/ppermute | solution.py:25
  288.9 9.2 %collective-permute-start.29 = (f32[2,5,128]{2,0,1:T(2,128)S(1)}, f32[2,5,128]{2,0,1:T(2,128)S(1)}, u32[]{:S(2)}, u32[]{:S(2)}) collective-permute-start(f32[2,5,128]{2,0,1:T(2,128)S(1)} %divide_add_fusion.1), channel_id=1, source_target_pairs={{1,0},{2,1},{3,2},{4,3},{5,4},{6,5},{7,6},{8,7},{9,8},{10,9},{11,1... | collective-permute-start | bytes 15368 | tf_op jit(solution)/shard_map/ppermute | solution.py:27
  330.5 5.3 %copy-start = (f32[2,5,4,8,128]{4,3,2,1,0:T(8,128)S(1)}, f32[2,5,4,8,128]{4,3,2,1,0:T(8,128)}, u32[]{:S(2)}) copy-start(f32[2,5,4,8,128]{4,3,2,1,0:T(8,128)} %param.9) | copy-start | bytes 491524
  330.5 6.2 %copy-start.4 = (f32[2]{0:T(128)S(1)}, f32[2]{0:T(128)}, u32[]{:S(2)}) copy-start(f32[2]{0:T(128)} %param.13) | copy-start | bytes 28
where the time goes:
time: 360 us; the launch traced here: 359 us
  starting transfers between devices  143 us (40%)
  local copies, waits for them, and re-layouts  92.3 us (26%)
  other arithmetic  57.3 us (16%)
  waiting for transfers between devices  28.7 us (8%)
  blocking collectives  21.3 us (6%)
  matrix products  14.3 us (4%)
    ppermute x15, starting transfers between devices, with_halo(): lax.ppermute(head, axis, [((i + 1) % count, i) for i in range(ends)])  113 us
    gather x2, local copies, waits for them, and re-layouts, local(): adjoint = adjoint + correction[:, :, local_ids].reshape(adjoint.shape)  57.1 us
    scatter-add x2, other arithmetic, local(): jax.ops.segment_sum(flattened.T, local_ids, num_segments=coarse_count)  48 us
    ppermute x15, starting transfers between devices, with_halo(): lax.ppermute(tail, axis, [(i, (i + 1) % count) for i in range(ends)])  29.3 us
    unnamed x1, blocking collectives  21.3 us
    ppermute x15, waiting for transfers between devices, with_halo(): lax.ppermute(head, axis, [((i + 1) % count, i) for i in range(ends)])  18.9 us
    gather x6, local copies, waits for them, and re-layouts, coarse_sweep(): neighbour_sum = jnp.sum(lookup[:, :, links], axis=2)  17 us
    dot_general x24, matrix products, operate(): jnp.einsum('cuv,cuxyz->cvxyz', jacobians[:, d], minus_one - plus_one, pre...  14.3 us
  transfers between devices with their start and end apart: 30, of which 21 were waited for; matrix products, arithmetic and copies ran while one was open for 1% of the time, Pallas kernels for 0%

commit v1 on v0

v1 whole, which is shorter than its diff:
```python
import functools

import jax
import jax.numpy as jnp
from jax import lax
from jax.experimental import pallas as pl
from jax.experimental.pallas import tpu as pltpu
from jax.sharding import PartitionSpec as P

RELAX = 0.7
EPS = 1.0 / 32.0
F32 = jnp.float32
STEP = 2


def sublanes(shape):
    return lax.broadcasted_iota(jnp.int32, shape, len(shape) - 2)


def lanes(shape):
    return lax.broadcasted_iota(jnp.int32, shape, len(shape) - 1)


def up(a, n):
    return pltpu.roll(a, 8 - n, a.ndim - 2)


def down(a, n):
    return pltpu.roll(a, n, a.ndim - 2)


def ahead(a, n):
    return pltpu.roll(a, 128 - n, a.ndim - 1)


def behind(a, n):
    return pltpu.roll(a, n, a.ndim - 1)


def pack(v):
    s, z = sublanes(v[0].shape), lanes(v[0].shape)
    even, low = s % 2 == 0, s % 4 < 2
    zeven, zlow = z % 2 == 0, z % 4 < 2

    def pair(a, b):
        return jnp.where(even, a, b) + jnp.where(even, up(a, 1), down(b, 1))

    def quad(a, b):
        return jnp.where(low, a, b) + jnp.where(low, up(a, 2), down(b, 2))

    four = quad(pair(v[0], v[1]), pair(v[2], v[3]))
    last = pair(v[4], v[4])
    last = quad(last, last)
    both = jnp.where(zeven, four, last) + jnp.where(zeven, ahead(four, 1), behind(last, 1))
    return both + jnp.where(zlow, ahead(both, 2), behind(both, 2))


def unpack(c):
    s, z = sublanes(c.shape), lanes(c.shape)
    even, low, zeven = s % 2 == 0, s % 4 < 2, z % 2 == 0
    four = jnp.where(zeven, c, behind(c, 1))
    last = jnp.where(zeven, ahead(c, 1), c)
    p02 = jnp.where(even, four, down(four, 1))
    p13 = jnp.where(even, up(four, 1), four)
    return (
        jnp.where(low, p02, down(p02, 2)),
        jnp.where(low, p13, down(p13, 2)),
        jnp.where(low, up(p02, 2), p02),
        jnp.where(low, up(p13, 2), p13),
        last,
    )


def coarse_solve(res, first, last_box, inverse):
    beta = 8.0 * inverse
    scaled = res * inverse
    c = scaled
    for sweep in range(1, 4):
        own = c[1:-1]
        at = first + sweep + lax.broadcasted_iota(jnp.int32, own.shape, 0)
        z = lanes(own.shape)
        total = jnp.where(at == 0, own, c[:-2]) + jnp.where(at == last_box, own, c[2:])
        total = total + (own + up(own, 4))
        total = total + jnp.where(z < 4, own, behind(own, 4)) + jnp.where(z >= 124, own, ahead(own, 4))
        c = scaled[sweep:-sweep] + beta * total
    return c


def off_diagonal(field, at, n, jac, cpx, cyz):
    shape = (n, 8, 128)
    s, z = sublanes(shape), lanes(shape)
    center = [field[u, pl.ds(at, n)] for u in range(5)]
    cx_plus, cx_minus = cpx[pl.ds(at - 1, n)], cpx[pl.ds(at - 2, n)]
    cy_plus, cy_minus, cz_plus, cz_minus = (cyz[i, pl.ds(at - 2, n)] for i in range(4))
    out = []
    diffs = []
    for u in range(5):
        a = center[u]
        plus, minus = field[u, pl.ds(at + 1, n)], field[u, pl.ds(at - 1, n)]
        far = field[u, pl.ds(at + 2, n)] + field[u, pl.ds(at - 2, n)]
        near = cx_plus * plus + cx_minus * minus
        dx = plus - minus
        plus, minus = up(a, 1), down(a, 1)
        far = far + jnp.where(s < 6, up(a, 2), 0.0) + jnp.where(s >= 2, down(a, 2), 0.0)
        near = near + (cy_plus * plus + cy_minus * minus)
        dy = jnp.where(s < 7, plus, 0.0) - jnp.where(s >= 1, minus, 0.0)
        plus, minus = ahead(a, 1), behind(a, 1)
        far = far + jnp.where(z < 126, ahead(a, 2), 0.0) + jnp.where(z >= 2, behind(a, 2), 0.0)
        near = near + (cz_plus * plus + cz_minus * minus)
        dz = jnp.where(z < 127, plus, 0.0) - jnp.where(z >= 1, minus, 0.0)
        out.append(near - EPS * far)
        diffs.append((dx, dy, dz))
    for v in range(5):
        for d in range(3):
            for u in range(5):
                out[v] = out[v] + jac[d * 25 + u * 5 + v] * diffs[u][d]
    return center, out


def kernel(
    n_cond, n_space, target_in, shape_in, jac_in, sensor_in, shift_in, weight_in, adjoint_out, sens_out,
    g, sen, shp, cpx, cyz, w, diag, jac, b0, b1, halo, rs, rp1, rp2, cs, rc, local_sem, send_sem, recv_sem,
):
    space, cond = lax.axis_index("space"), lax.axis_index("cond")
    chip, core = space // 2, space % 2
    chips = n_space // 2
    has_left, has_right = chip > 0, chip < chips - 1
    has_left2, has_right2 = chip > 1, chip < chips - 2
    rows = 8 // n_cond

    barrier = pltpu.get_barrier_semaphore()
    peers = [(2 * chip + 1 - core, cond, None)]
    for near, there in ((-1, has_left), (1, has_right)):
        peers += [(2 * (chip + near) + j, cond, there) for j in range(2)]
    for far, there in ((-2, has_left2), (2, has_right2)):
        peers.append((2 * (chip + far) + core, cond, there))
    ring = [(2 * chip + (core + j) % 2, lax.rem(cond + dz, n_cond)) for dz in range(n_cond) for j in range(2)]
    peers += [(s, c, None) for s, c in ring[2:]]
    for s, c, there in peers:
        def greet(s=s, c=c):
            pl.semaphore_signal(barrier, inc=1, device_id={"space": s, "cond": c})
        greet() if there is None else pl.when(there)(greet)

    count = iter(range(1000))
    sends = []

    def remote(src, dst, recv, s, c=cond):
        return pltpu.make_async_remote_copy(
            src_ref=src, dst_ref=dst, send_sem=send_sem.at[next(count)], recv_sem=recv_sem.at[recv],
            device_id={"space": s, "cond": c},
        )

    mine = [
        pltpu.make_async_copy(target_in.at[core], g.at[:, pl.ds(6 + 4 * core, 4)], local_sem.at[0]),
        pltpu.make_async_copy(sensor_in.at[core], sen.at[pl.ds(7 + 4 * core, 4)], local_sem.at[1]),
        pltpu.make_async_copy(shape_in.at[core], shp.at[:, pl.ds(4 * core, 4)], local_sem.at[2]),
    ]
    for copy in mine:
        copy.start()

    @pl.when(jnp.logical_not(has_left))
    def _():
        g[:, 0:6] = jnp.zeros((5, 6, 8, 128), F32)
        sen[0:7] = jnp.zeros((7, 8, 128), F32)
        halo[:, 0:6] = jnp.zeros((5, 6, 8, 128), F32)
        rp1[3:7] = jnp.zeros((4, 8, 128), F32)
        rp2[0:3] = jnp.zeros((3, 8, 128), F32)

    @pl.when(jnp.logical_not(has_right))
    def _():
        g[:, 14:20] = jnp.zeros((5, 6, 8, 128), F32)
        sen[15:22] = jnp.zeros((7, 8, 128), F32)
        halo[:, 6:12] = jnp.zeros((5, 6, 8, 128), F32)
        rp1[11:15] = jnp.zeros((4, 8, 128), F32)
        rp2[7:10] = jnp.zeros((3, 8, 128), F32)

    @pl.when(jnp.logical_not(has_left2))
    def _():
        rp1[0:3] = jnp.zeros((3, 8, 128), F32)

    @pl.when(jnp.logical_not(has_right2))
    def _():
        rp1[15:18] = jnp.zeros((3, 8, 128), F32)

    for d in range(3):
        for u in range(5):
            for v in range(5):
                jac[d * 25 + u * 5 + v] = jnp.full((8, 128), 0.5 * jac_in[core, d, u, v], F32)
    shift = jnp.full((8, 128), shift_in[core], F32)
    inverse = 1.0 / (shift * 32.0 + 48.0)

    n_peers = 1 + 2 * (n_cond - 1)
    pl.semaphore_wait(
        barrier,
        n_peers + 2 * has_left.astype(jnp.int32) + 2 * has_right.astype(jnp.int32)
        + has_left2.astype(jnp.int32) + has_right2.astype(jnp.int32),
    )

    def to_right(k, j):
        low, size, at = ((2, 2, 0), (0, 4, 2))[k]
        s_low, s_size, s_at = ((1, 3, 0), (0, 4, 3))[k]
        there = 2 * (chip + 1) + j
        return [
            remote(sensor_in.at[j, pl.ds(s_low, s_size)], sen.at[pl.ds(s_at, s_size)], 3 + 2 * k, there),
            remote(target_in.at[j, :, pl.ds(low, size)], g.at[:, pl.ds(at, size)], 4 + 2 * k, there),
        ]

    def to_left(k, j):
        size, at = ((4, 14), (2, 18))[k]
        s_size, s_at = ((4, 15), (3, 19))[k]
        there = 2 * (chip - 1) + j
        return [
            remote(sensor_in.at[j, pl.ds(0, s_size)], sen.at[pl.ds(s_at, s_size)], 7 + 2 * k, there),
            remote(target_in.at[j, :, pl.ds(0, size)], g.at[:, pl.ds(at, size)], 8 + 2 * k, there),
        ]

    first_round = []
    for k in range(2):
        for j in range(2):
            for make, there in ((to_right, has_right), (to_left, has_left)):
                first_round.append((make(k, j), jnp.logical_and(there, core == k)))
    for copies, there in first_round:
        @pl.when(there)
        def _(copies=copies):
            for copy in copies:
                copy.start()
    other = 1 - core
    sibling = 2 * chip + other
    swap = [
        remote(sensor_in.at[other], sen.at[pl.ds(7 + 4 * core, 4)], 0, sibling),
        remote(target_in.at[other], g.at[:, pl.ds(6 + 4 * core, 4)], 1, sibling),
        remote(shape_in.at[other], shp.at[:, pl.ds(4 * core, 4)], 2, sibling),
    ]
    for copy in swap:
        copy.start()

    for copy in mine:
        copy.wait()
    for copy in swap:
        copy.wait_recv()
    for k in range(2):
        for make, there in ((to_right, has_left), (to_left, has_right)):
            copies = make(k, 0)

            @pl.when(there)
            def _(copies=copies):
                for copy in copies:
                    copy.wait_recv()

    s, z = sublanes((1, 8, 128)), lanes((1, 8, 128))

    def coefficients(i, carry):
        near = sen[pl.ds(i + 1, 1)]
        x_plus, x_minus = (near + sen[pl.ds(i + 2, 1)]) * 0.25, (near + sen[pl.ds(i, 1)]) * 0.25
        y_plus = (near + jnp.where(s < 7, up(near, 1), 0.0)) * 0.25
        y_minus = (near + jnp.where(s >= 1, down(near, 1), 0.0)) * 0.25
        z_plus = (near + jnp.where(z < 127, ahead(near, 1), 0.0)) * 0.25
        z_minus = (near + jnp.where(z >= 1, behind(near, 1), 0.0)) * 0.25
        total = shift[None] + ((x_plus + x_minus) + (y_plus + y_minus) + (z_plus + z_minus)) + 18.0 * EPS
        cpx[pl.ds(i + 1, 1)] = x_plus + 4.0 * EPS
        cyz[0, pl.ds(i, 1)] = jnp.where(s < 7, y_plus + 4.0 * EPS, 0.0)
        cyz[1, pl.ds(i, 1)] = jnp.where(s >= 1, y_minus + 4.0 * EPS, 0.0)
        cyz[2, pl.ds(i, 1)] = jnp.where(z < 127, z_plus + 4.0 * EPS, 0.0)
        cyz[3, pl.ds(i, 1)] = jnp.where(z >= 1, z_minus + 4.0 * EPS, 0.0)
        inside = jnp.logical_and(jnp.logical_or(has_left, i >= 6), jnp.logical_or(has_right, i < 14))
        weight = jnp.where(inside, RELAX / total, 0.0)
        diag[pl.ds(i, 1)] = total
        w[pl.ds(i, 1)] = weight
        for v in range(5):
            b0[v, pl.ds(i + 2, 1)] = weight * g[v, pl.ds(i, 1)]
        return carry

    cpx[0:1] = (sen[0:1] + sen[1:2]) * 0.25 + 4.0 * EPS
    lax.fori_loop(0, 20, coefficients, 0)

    def sweep(src, dst, low, high):
        def body(i, carry):
            at = low + i * STEP
            center, out = off_diagonal(src, at, STEP, jac, cpx, cyz)
            weight = w[pl.ds(at - 2, STEP)]
            for v in range(5):
                dst[v, pl.ds(at, STEP)] = (1.0 - RELAX) * center[v] + weight * (g[v, pl.ds(at - 2, STEP)] + out[v])
            return carry

        lax.fori_loop(0, (high - low) // STEP, body, 0)

    def restrict(src):
        def body(i, carry):
            at = 8 + i * 2
            center, out = off_diagonal(src, at, 2, jac, cpx, cyz)
            d = diag[pl.ds(at - 2, 2)]
            for v in range(5):
                r = g[v, pl.ds(at - 2, 2)] + out[v] - d * center[v]
                rs[v, pl.ds(i, 1)] = r[0:1] + r[1:2]
            return carry

        lax.fori_loop(0, 4, body, 0)
        return pack([rs[v] for v in range(5)])

    right, left = space + 2, space - 2

    def start(copies):
        for copy, there in copies:
            pl.when(there)(copy.start)

    def arrive(copies, theres):
        for (copy, _), there in zip(copies, theres):
            pl.when(there)(copy.wait_recv)

    def sent(copies):
        for copy, there in copies:
            pl.when(there)(copy.wait_send)

    sweep(b0, b1, 4, 20)
    sweep(b1, b0, 6, 18)
    halos = [
        (remote(b0.at[:, pl.ds(8, 6)], halo.at[:, pl.ds(0, 6)], 11, right), has_right),
        (remote(b0.at[:, pl.ds(10, 6)], halo.at[:, pl.ds(6, 6)], 12, left), has_left),
    ]
    start(halos)
    rp1[7:11] = restrict(b0)
    boxes = [
        (remote(rp1.at[pl.ds(8, 3)], rp1.at[pl.ds(0, 3)], 13, space + 4), has_right2),
        (remote(rp1.at[pl.ds(7, 3)], rp1.at[pl.ds(15, 3)], 14, space - 4), has_left2),
        (remote(rp1.at[pl.ds(7, 4)], rp1.at[pl.ds(3, 4)], 15, right), has_right),
        (remote(rp1.at[pl.ds(7, 4)], rp1.at[pl.ds(11, 4)], 16, left), has_left),
    ]
    start(boxes)
    arrive(halos, (has_left, has_right))
    arrive(boxes, (has_left2, has_right2, has_left, has_right))
    last_box = 4 * chips - 1
    c = coarse_solve(rp1[...], 4 * chip - 7, last_box, inverse[None])
    at = 4 * chip - 4 + lax.broadcasted_iota(jnp.int32, c.shape, 0)
    c = jnp.where(jnp.logical_and(at >= 0, at <= last_box), c, 0.0)
    rs1 = unpack(c)
    for v in range(5):
        for i in range(12):
            add = rs1[v][i]
            for j in (2 * i, 2 * i + 1):
                old = halo[v, j] if j < 6 else b0[v, j] if j < 18 else halo[v, j - 12]
                b1[v, j] = old + add
    sent(halos)

    sweep(b1, b0, 2, 22)
    sweep(b0, b1, 4, 20)
    sweep(b1, b0, 6, 18)
    rp2[3:7] = restrict(b0)
    boxes2 = [
        (remote(rp2.at[pl.ds(4, 3)], rp2.at[pl.ds(0, 3)], 17, right), has_right),
        (remote(rp2.at[pl.ds(3, 3)], rp2.at[pl.ds(7, 3)], 18, left), has_left),
    ]
    start(boxes2)
    arrive(boxes2, (has_left, has_right))
    c = coarse_solve(rp2[...], 4 * chip - 3, last_box, inverse[None])
    fixes = unpack(c)
    weight = jnp.full((8, 128), weight_in[core], F32)
    parts = []
    for i in range(8):
        total = None
        for v in range(5):
            new = b0[v, 8 + i] + fixes[v][i // 2]
            b1[v, 8 + i] = new
            term = new * shp[v, i]
            total = term if total is None else total + term
        parts.append(weight * total)

    s2 = sublanes((8, 128))
    for j in range(2):
        for c_to in range(n_cond):
            gathered = None
            for i in range(4):
                turn = (rows * i - rows * c_to) % 8
                moved = parts[4 * j + i] if turn == 0 else down(parts[4 * j + i], turn)
                gathered = moved if gathered is None else jnp.where(s2 >= rows * i, moved, gathered)
            cs[j * n_cond + c_to] = gathered
    me = 2 * cond + core
    shares = []
    for i, (s_to, c_to) in enumerate(ring[1:]):
        shares.append(remote(cs.at[lax.rem(s_to, 2) * n_cond + c_to], rc.at[me], 19 + i, s_to, c_to))
    for copy in reversed(shares):
        copy.start()
    back = remote(b1.at[:, pl.ds(8 + 4 * other, 4)], adjoint_out.at[core], 26, sibling)
    back.start()
    keep = pltpu.make_async_copy(b1.at[:, pl.ds(8 + 4 * core, 4)], adjoint_out.at[core], local_sem.at[0])
    keep.start()
    rc[me] = cs[core * n_cond + cond]
    for copy in shares:
        copy.wait_recv()
    total = rc[0]
    for i in range(1, 2 * n_cond):
        total = total + rc[i]
    for i in range(4):
        sens_out[i] = total[rows * i : rows * (i + 1)]
    keep.wait()
    back.wait()
    for copy in shares:
        copy.wait_send()
    for copy in swap:
        copy.wait_send()
    for copies, there in first_round:
        @pl.when(there)
        def _(copies=copies):
            for copy in copies:
                copy.wait_send()
    sent(boxes)
    sent(boxes2)


def solution(mesh):
    n_cond, n_space = mesh.shape["cond"], mesh.shape["space"]
    rows = 8 // n_cond

    def local(target, shape, jac, sensor, shift, weight, agglomeration, links):
        vmem = lambda *shape: pltpu.VMEM((*shape, 8, 128), F32)
        hbm = pl.BlockSpec(memory_space=pl.ANY)
        smem = pl.BlockSpec(memory_space=pltpu.SMEM)
        return pl.pallas_call(
            functools.partial(kernel, n_cond, n_space),
            out_shape=(
                jax.ShapeDtypeStruct(target.shape, F32),
                jax.ShapeDtypeStruct((4, rows, 128), F32),
            ),
            in_specs=[hbm, hbm, smem, hbm, smem, smem],
            out_specs=(hbm, pl.BlockSpec(memory_space=pltpu.VMEM)),
            scratch_shapes=[
                vmem(5, 20), vmem(22), vmem(5, 8),
                vmem(21), vmem(4, 20), vmem(20), vmem(20), vmem(75),
                vmem(5, 24), vmem(5, 24), vmem(5, 12), vmem(5, 4),
                vmem(18), vmem(10), vmem(2 * n_cond), vmem(2 * n_cond),
                pltpu.SemaphoreType.DMA((3,)),
                pltpu.SemaphoreType.DMA((64,)),
                pltpu.SemaphoreType.DMA((27,)),
            ],
            compiler_params=pltpu.CompilerParams(
                collective_id=0, has_side_effects=True, vmem_limit_bytes=48 * 2**20
            ),
        )(target, shape, jac, sensor, shift, weight)

    in_specs = (
        P("cond", None, "space", None, None),
        P("cond", None, "space", None, None),
        P("cond", None, None, None),
        P("cond", "space", None, None),
        P("cond"),
        P("cond"),
        P("space", None, None),
        P(None, "space"),
    )
    out_specs = (P("cond", None, "space", None, None), P("space", "cond", None))
    return jax.shard_map(local, mesh=mesh, in_specs=in_specs, out_specs=out_specs, check_vma=False)
```

time: 360 us -> 46.4 us (0.13)
  the two profiles are of different devices: /device:TPU:32 before, /device:TPU:30 now
where the time goes in v1:
time: 46.4 us; the launch traced here: 46.3 us
  Pallas kernels  41.7 us (90%)
  local copies, waits for them, and re-layouts  3.86 us (8%)
  between operations  0.67 us (1%)
    pallas_call x1, Pallas kernels, local(): pl.pallas_call(functools.partial(kernel, n_cond, n_space), out_shape=(jax...  41.7 us
    unnamed x13, local copies, waits for them, and re-layouts  3.86 us

profile of v1, /device:TPU:30, one launch (start us, length us, event | category | flops | bytes accessed | tf_op | source)
XLA Modules:
  0.0 46.3 jit_solution(2699216956042248157)
XLA Ops:
  0.6 0.0 copy-start.4
  0.6 0.0 copy-start.3
  0.7 0.0 copy-start.2
  0.7 0.7 %copy.8.jac_in = f32[2,3,5,5]{3,2,1,0:T(8,128)S(1)} copy(f32[2,3,5,5]{3,0,2,1:T(2,128)} %param.10) | data formatting | bytes 1200 | tf_op args[2]
  1.4 0.0 copy-done.4
  1.4 0.0 copy-done.3
  1.4 0.0 copy-done.2
  1.4 0.0 copy-start
  1.4 0.9 %copy-done = f32[2,5,4,8,128]{4,3,2,1,0:T(8,128)S(1)} copy-done((f32[2,5,4,8,128]{4,3,2,1,0:T(8,128)S(1)}, f32[2,5,4,8,128]{4,3,2,1,0:T(8,128)}, u32[]{:S(2)}) %copy-start) | copy-done | bytes 163864
  2.3 0.0 copy-start.1
  2.3 0.9 %copy-done.1 = f32[2,5,4,8,128]{4,3,2,1,0:T(8,128)S(1)} copy-done((f32[2,5,4,8,128]{4,3,2,1,0:T(8,128)S(1)}, f32[2,5,4,8,128]{4,3,2,1,0:T(8,128)}, u32[]{:S(2)}) %copy-start.1) | copy-done | bytes 163864
  3.3 41.7 %shard_map.77 = (f32[2,5,4,8,128]{4,3,2,1,0:T(8,128)S(1)}, f32[4,2,128]{2,1,0:T(2,128)S(1)}) custom-call(f32[2,5,4,8,128]{4,3,2,1,0:T(8,128)S(1)} %copy-done, f32[2,5,4,8,128]{4,3,2,1,0:T(8,128)S(1)} %copy-done.1, f32[2,3,5,5]{3,2,1,0:T(8,128)S(1)} %copy.8.jac_in, f32[2,4,8,128]{3,2,1,0:T(8,128)S(1)} %copy-done.2, f32[2]{0:T(128)S(1)} %copy-done.3, ...), custom_call_target="tpu_custom_call" | custom-call | tf_op jit(solution)/shard_map/pallas_call | solution.py:417
  45.0 0.7 %copy.11 = f32[2,5,4,8,128]{4,3,2,1,0:T(8,128)} copy(f32[2,5,4,8,128]{4,3,2,1,0:T(8,128)S(1)} %get-tuple-element.4) | data formatting | bytes 327680
  45.7 0.6 %copy.12 = f32[4,2,128]{2,1,0:T(2,128)} copy(f32[4,2,128]{2,1,0:T(2,128)S(1)} %get-tuple-element.5) | data formatting | bytes 8192
Async XLA Ops:
  0.6 0.8 %copy-start.4 = (f32[2]{0:T(128)S(1)}, f32[2]{0:T(128)}, u32[]{:S(2)}) copy-start(f32[2]{0:T(128)} %weight_in.1) | copy-start | bytes 28
  0.6 0.8 %copy-start.3 = (f32[2]{0:T(128)S(1)}, f32[2]{0:T(128)}, u32[]{:S(2)}) copy-start(f32[2]{0:T(128)} %shift_in.1) | copy-start | bytes 28
  0.7 0.8 %copy-start.2 = (f32[2,4,8,128]{3,2,1,0:T(8,128)S(1)}, f32[2,4,8,128]{3,2,1,0:T(8,128)}, u32[]{:S(2)}) copy-start(f32[2,4,8,128]{3,2,1,0:T(8,128)} %sensor_in.1) | copy-start | bytes 98308
  1.4 0.9 %copy-start = (f32[2,5,4,8,128]{4,3,2,1,0:T(8,128)S(1)}, f32[2,5,4,8,128]{4,3,2,1,0:T(8,128)}, u32[]{:S(2)}) copy-start(f32[2,5,4,8,128]{4,3,2,1,0:T(8,128)} %target_in.1) | copy-start | bytes 491524
  2.3 0.9 %copy-start.1 = (f32[2,5,4,8,128]{4,3,2,1,0:T(8,128)S(1)}, f32[2,5,4,8,128]{4,3,2,1,0:T(8,128)}, u32[]{:S(2)}) copy-start(f32[2,5,4,8,128]{4,3,2,1,0:T(8,128)} %shape_in.1) | copy-start | bytes 491524

commit v2 on v1

--- a/solution.py
+++ b/solution.py
@@ -10,7 +10,6 @@
 RELAX = 0.7
 EPS = 1.0 / 32.0
 F32 = jnp.float32
-STEP = 2
 
 
 def sublanes(shape):
@@ -87,39 +86,48 @@
 
 
 def off_diagonal(field, at, n, jac, cpx, cyz):
-    shape = (n, 8, 128)
-    s, z = sublanes(shape), lanes(shape)
-    center = [field[u, pl.ds(at, n)] for u in range(5)]
-    cx_plus, cx_minus = cpx[pl.ds(at - 1, n)], cpx[pl.ds(at - 2, n)]
+    s, z = sublanes((1, 8, 128)), lanes((1, 8, 128))
+    y_not_last, y_not_first = jnp.where(s < 7, 1.0, 0.0), jnp.where(s >= 1, 1.0, 0.0)
+    z_not_last, z_not_first = jnp.where(z < 127, 1.0, 0.0), jnp.where(z >= 1, 1.0, 0.0)
+    y_far_up, y_far_down = jnp.where(s < 6, -EPS, 0.0), jnp.where(s >= 2, -EPS, 0.0)
+    z_far_up, z_far_down = jnp.where(z < 126, -EPS, 0.0), jnp.where(z >= 2, -EPS, 0.0)
+    cx = cpx[pl.ds(at - 2, n + 1)]
     cy_plus, cy_minus, cz_plus, cz_minus = (cyz[i, pl.ds(at - 2, n)] for i in range(4))
-    out = []
-    diffs = []
+    center, out = [], [None] * 5
+
+    def add(v, term):
+        out[v] = term if out[v] is None else out[v] + term
+
     for u in range(5):
-        a = center[u]
-        plus, minus = field[u, pl.ds(at + 1, n)], field[u, pl.ds(at - 1, n)]
-        far = field[u, pl.ds(at + 2, n)] + field[u, pl.ds(at - 2, n)]
-        near = cx_plus * plus + cx_minus * minus
+        block = field[u, pl.ds(at - 2, n + 4)]
+        a, plus, minus = block[2:-2], block[3:-1], block[1:-3]
+        center.append(a)
+        total = cx[1:] * plus
+        total = total + cx[:-1] * minus
+        total = total - EPS * (block[4:] + block[:-4])
         dx = plus - minus
         plus, minus = up(a, 1), down(a, 1)
-        far = far + jnp.where(s < 6, up(a, 2), 0.0) + jnp.where(s >= 2, down(a, 2), 0.0)
-        near = near + (cy_plus * plus + cy_minus * minus)
-        dy = jnp.where(s < 7, plus, 0.0) - jnp.where(s >= 1, minus, 0.0)
+        total = total + cy_plus * plus
+        total = total + cy_minus * minus
+        total = total + y_far_up * up(a, 2)
+        total = total + y_far_down * down(a, 2)
+        dy = y_not_last * plus - y_not_first * minus
         plus, minus = ahead(a, 1), behind(a, 1)
-        far = far + jnp.where(z < 126, ahead(a, 2), 0.0) + jnp.where(z >= 2, behind(a, 2), 0.0)
-        near = near + (cz_plus * plus + cz_minus * minus)
-        dz = jnp.where(z < 127, plus, 0.0) - jnp.where(z >= 1, minus, 0.0)
-        out.append(near - EPS * far)
-        diffs.append((dx, dy, dz))
-    for v in range(5):
-        for d in range(3):
-            for u in range(5):
-                out[v] = out[v] + jac[d * 25 + u * 5 + v] * diffs[u][d]
+        total = total + cz_plus * plus
+        total = total + cz_minus * minus
+        total = total + z_far_up * ahead(a, 2)
+        total = total + z_far_down * behind(a, 2)
+        dz = z_not_last * plus - z_not_first * minus
+        add(u, total)
+        for d, diff in enumerate((dx, dy, dz)):
+            for v in range(5):
+                add(v, jac[d * 25 + u * 5 + v] * diff)
     return center, out
 
 
 def kernel(
-    n_cond, n_space, target_in, shape_in, jac_in, sensor_in, shift_in, weight_in, adjoint_out, sens_out,
-    g, sen, shp, cpx, cyz, w, diag, jac, b0, b1, halo, rs, rp1, rp2, cs, rc, local_sem, send_sem, recv_sem,
+    n_cond, n_space, target_in, shape_in, jac_hbm, sensor_in, shift_hbm, weight_hbm, adjoint_out, sens_out,
+    jac_in, shift_in, weight_in, g, sen, shp, cpx, cyz, w, diag, jac, b0, b1, b2, halo, rs, rp1, rp2, cs, rc, local_sem, send_sem, recv_sem,
 ):
     space, cond = lax.axis_index("space"), lax.axis_index("cond")
     chip, core = space // 2, space % 2
@@ -151,11 +159,16 @@
         )
 
     mine = [
-        pltpu.make_async_copy(target_in.at[core], g.at[:, pl.ds(6 + 4 * core, 4)], local_sem.at[0]),
-        pltpu.make_async_copy(sensor_in.at[core], sen.at[pl.ds(7 + 4 * core, 4)], local_sem.at[1]),
+        pltpu.make_async_copy(sensor_in.at[core], sen.at[pl.ds(7 + 4 * core, 4)], local_sem.at[0]),
+        pltpu.make_async_copy(target_in.at[core], g.at[:, pl.ds(6 + 4 * core, 4)], local_sem.at[1]),
         pltpu.make_async_copy(shape_in.at[core], shp.at[:, pl.ds(4 * core, 4)], local_sem.at[2]),
     ]
-    for copy in mine:
+    small = [
+        pltpu.make_async_copy(jac_hbm, jac_in, local_sem.at[3]),
+        pltpu.make_async_copy(shift_hbm, shift_in, local_sem.at[4]),
+        pltpu.make_async_copy(weight_hbm, weight_in, local_sem.at[5]),
+    ]
+    for copy in small + mine:
         copy.start()
 
     @pl.when(jnp.logical_not(has_left))
@@ -182,10 +195,12 @@
     def _():
         rp1[15:18] = jnp.zeros((3, 8, 128), F32)
 
+    for copy in small:
+        copy.wait()
     for d in range(3):
         for u in range(5):
             for v in range(5):
-                jac[d * 25 + u * 5 + v] = jnp.full((8, 128), 0.5 * jac_in[core, d, u, v], F32)
+                jac[d * 25 + u * 5 + v] = jnp.full((8, 128), 0.5 * jac_in[d, u, core, v], F32)
     shift = jnp.full((8, 128), shift_in[core], F32)
     inverse = 1.0 / (shift * 32.0 + 48.0)
 
@@ -216,14 +231,9 @@
 
     first_round = []
     for k in range(2):
-        for j in range(2):
-            for make, there in ((to_right, has_right), (to_left, has_left)):
-                first_round.append((make(k, j), jnp.logical_and(there, core == k)))
-    for copies, there in first_round:
-        @pl.when(there)
-        def _(copies=copies):
-            for copy in copies:
-                copy.start()
+        for make, there in ((to_right, has_right), (to_left, has_left)):
+            pairs = [make(k, j) for j in range(2)]
+            first_round.append(([c[0] for c in pairs] + [c[1] for c in pairs], jnp.logical_and(there, core == k)))
     other = 1 - core
     sibling = 2 * chip + other
     swap = [
@@ -231,70 +241,84 @@
         remote(target_in.at[other], g.at[:, pl.ds(6 + 4 * core, 4)], 1, sibling),
         remote(shape_in.at[other], shp.at[:, pl.ds(4 * core, 4)], 2, sibling),
     ]
+    for copies, there in first_round:
+        @pl.when(there)
+        def _(copies=copies):
+            for copy in copies:
+                copy.start()
     for copy in swap:
         copy.start()
 
-    for copy in mine:
-        copy.wait()
-    for copy in swap:
-        copy.wait_recv()
-    for k in range(2):
-        for make, there in ((to_right, has_left), (to_left, has_right)):
-            copies = make(k, 0)
-
-            @pl.when(there)
-            def _(copies=copies):
-                for copy in copies:
-                    copy.wait_recv()
+    awaited = [(make(k, 0), there) for k in range(2) for make, there in ((to_right, has_left), (to_left, has_right))]
+
+    def arrive_first(i):
+        mine[i].wait()
+        swap[i].wait_recv()
+        for copies, there in awaited:
+            pl.when(there)(copies[i].wait_recv)
+
+    arrive_first(0)
 
     s, z = sublanes((1, 8, 128)), lanes((1, 8, 128))
 
-    def coefficients(i, carry):
-        near = sen[pl.ds(i + 1, 1)]
-        x_plus, x_minus = (near + sen[pl.ds(i + 2, 1)]) * 0.25, (near + sen[pl.ds(i, 1)]) * 0.25
+    def coefficients(k, carry):
+        i = 4 * k
+        block = sen[pl.ds(i, 6)]
+        near = block[1:5]
+        x_plus, x_minus = (near + block[2:]) * 0.25, (near + block[:4]) * 0.25
         y_plus = (near + jnp.where(s < 7, up(near, 1), 0.0)) * 0.25
         y_minus = (near + jnp.where(s >= 1, down(near, 1), 0.0)) * 0.25
         z_plus = (near + jnp.where(z < 127, ahead(near, 1), 0.0)) * 0.25
         z_minus = (near + jnp.where(z >= 1, behind(near, 1), 0.0)) * 0.25
         total = shift[None] + ((x_plus + x_minus) + (y_plus + y_minus) + (z_plus + z_minus)) + 18.0 * EPS
-        cpx[pl.ds(i + 1, 1)] = x_plus + 4.0 * EPS
-        cyz[0, pl.ds(i, 1)] = jnp.where(s < 7, y_plus + 4.0 * EPS, 0.0)
-        cyz[1, pl.ds(i, 1)] = jnp.where(s >= 1, y_minus + 4.0 * EPS, 0.0)
-        cyz[2, pl.ds(i, 1)] = jnp.where(z < 127, z_plus + 4.0 * EPS, 0.0)
-        cyz[3, pl.ds(i, 1)] = jnp.where(z >= 1, z_minus + 4.0 * EPS, 0.0)
-        inside = jnp.logical_and(jnp.logical_or(has_left, i >= 6), jnp.logical_or(has_right, i < 14))
-        weight = jnp.where(inside, RELAX / total, 0.0)
-        diag[pl.ds(i, 1)] = total
-        w[pl.ds(i, 1)] = weight
+        cpx[pl.ds(i + 1, 4)] = x_plus + 4.0 * EPS
+        cyz[0, pl.ds(i, 4)] = jnp.where(s < 7, y_plus + 4.0 * EPS, 0.0)
+        cyz[1, pl.ds(i, 4)] = jnp.where(s >= 1, y_minus + 4.0 * EPS, 0.0)
+        cyz[2, pl.ds(i, 4)] = jnp.where(z < 127, z_plus + 4.0 * EPS, 0.0)
+        cyz[3, pl.ds(i, 4)] = jnp.where(z >= 1, z_minus + 4.0 * EPS, 0.0)
+        at = i + lax.broadcasted_iota(jnp.int32, total.shape, 0)
+        inside = jnp.logical_and(at >= low_layer, at < high_layer)
+        diag[pl.ds(i, 4)] = total
+        w[pl.ds(i, 4)] = jnp.where(inside, RELAX / total, 0.0)
+        return carry
+
+    low_layer, high_layer = jnp.where(has_left, 0, 6), jnp.where(has_right, 20, 14)
+    cpx[0:1] = (sen[0:1] + sen[1:2]) * 0.25 + 4.0 * EPS
+    lax.fori_loop(0, 5, coefficients, 0)
+    arrive_first(1)
+
+    def begin(k, carry):
+        i = 4 * k
+        weight = w[pl.ds(i, 4)]
         for v in range(5):
-            b0[v, pl.ds(i + 2, 1)] = weight * g[v, pl.ds(i, 1)]
+            b0[v, pl.ds(i + 2, 4)] = weight * g[v, pl.ds(i, 4)]
         return carry
 
-    cpx[0:1] = (sen[0:1] + sen[1:2]) * 0.25 + 4.0 * EPS
-    lax.fori_loop(0, 20, coefficients, 0)
-
-    def sweep(src, dst, low, high):
+    lax.fori_loop(0, 5, begin, 0)
+
+    def sweep(src, dst, low, n, times, stride=None):
         def body(i, carry):
-            at = low + i * STEP
-            center, out = off_diagonal(src, at, STEP, jac, cpx, cyz)
-            weight = w[pl.ds(at - 2, STEP)]
+            at = low + i * (stride or n)
+            center, out = off_diagonal(src, at, n, jac, cpx, cyz)
+            weight = w[pl.ds(at - 2, n)]
             for v in range(5):
-                dst[v, pl.ds(at, STEP)] = (1.0 - RELAX) * center[v] + weight * (g[v, pl.ds(at - 2, STEP)] + out[v])
+                dst[v, pl.ds(at, n)] = (1.0 - RELAX) * center[v] + weight * (g[v, pl.ds(at - 2, n)] + out[v])
             return carry
 
-        lax.fori_loop(0, (high - low) // STEP, body, 0)
+        lax.fori_loop(0, times, body, 0)
 
     def restrict(src):
         def body(i, carry):
-            at = 8 + i * 2
-            center, out = off_diagonal(src, at, 2, jac, cpx, cyz)
-            d = diag[pl.ds(at - 2, 2)]
+            at = 8 + i * 4
+            center, out = off_diagonal(src, at, 4, jac, cpx, cyz)
+            d = diag[pl.ds(at - 2, 4)]
             for v in range(5):
-                r = g[v, pl.ds(at - 2, 2)] + out[v] - d * center[v]
-                rs[v, pl.ds(i, 1)] = r[0:1] + r[1:2]
+                r = g[v, pl.ds(at - 2, 4)] + out[v] - d * center[v]
+                rs[v, pl.ds(2 * i, 1)] = r[0:1] + r[1:2]
+                rs[v, pl.ds(2 * i + 1, 1)] = r[2:3] + r[3:4]
             return carry
 
-        lax.fori_loop(0, 4, body, 0)
+        lax.fori_loop(0, 2, body, 0)
         return pack([rs[v] for v in range(5)])
 
     right, left = space + 2, space - 2
@@ -311,13 +335,17 @@
         for copy, there in copies:
             pl.when(there)(copy.wait_send)
 
-    sweep(b0, b1, 4, 20)
-    sweep(b1, b0, 6, 18)
-    halos = [
-        (remote(b0.at[:, pl.ds(8, 6)], halo.at[:, pl.ds(0, 6)], 11, right), has_right),
-        (remote(b0.at[:, pl.ds(10, 6)], halo.at[:, pl.ds(6, 6)], 12, left), has_left),
-    ]
-    start(halos)
+    sweep(b0, b1, 4, 4, 4)
+    sweep(b1, b0, 6, 4, 3)
+    near_halos = [
+        (remote(b0.at[:, pl.ds(12, 2)], halo.at[:, pl.ds(4, 2)], 11, right), has_right),
+        (remote(b0.at[:, pl.ds(10, 2)], halo.at[:, pl.ds(6, 2)], 12, left), has_left),
+    ]
+    far_halos = [
+        (remote(b0.at[:, pl.ds(8, 4)], halo.at[:, pl.ds(0, 4)], 19, right), has_right),
+        (remote(b0.at[:, pl.ds(12, 4)], halo.at[:, pl.ds(8, 4)], 20, left), has_left),
+    ]
+    start(near_halos)
     rp1[7:11] = restrict(b0)
     boxes = [
         (remote(rp1.at[pl.ds(8, 3)], rp1.at[pl.ds(0, 3)], 13, space + 4), has_right2),
@@ -326,25 +354,27 @@
         (remote(rp1.at[pl.ds(7, 4)], rp1.at[pl.ds(11, 4)], 16, left), has_left),
     ]
     start(boxes)
-    arrive(halos, (has_left, has_right))
+    start(far_halos)
     arrive(boxes, (has_left2, has_right2, has_left, has_right))
     last_box = 4 * chips - 1
     c = coarse_solve(rp1[...], 4 * chip - 7, last_box, inverse[None])
     at = 4 * chip - 4 + lax.broadcasted_iota(jnp.int32, c.shape, 0)
-    c = jnp.where(jnp.logical_and(at >= 0, at <= last_box), c, 0.0)
-    rs1 = unpack(c)
-    for v in range(5):
-        for i in range(12):
-            add = rs1[v][i]
-            for j in (2 * i, 2 * i + 1):
-                old = halo[v, j] if j < 6 else b0[v, j] if j < 18 else halo[v, j - 12]
-                b1[v, j] = old + add
-    sent(halos)
-
-    sweep(b1, b0, 2, 22)
-    sweep(b0, b1, 4, 20)
-    sweep(b1, b0, 6, 18)
-    rp2[3:7] = restrict(b0)
+    fixes = unpack(jnp.where(jnp.logical_and(at >= 0, at <= last_box), c, 0.0))
+
+    def correct(old, low, high):
+        for v in range(5):
+            for i in range(low, high):
+                b1[v, i] = old(v, i) + fixes[v][i // 2]
+
+    correct(lambda v, i: b0[v, i], 6, 18)
+    sweep(b1, b2, 8, 4, 2)
+    arrive(near_halos + far_halos, (has_left, has_right) * 2)
+    correct(lambda v, i: halo[v, i], 0, 6)
+    correct(lambda v, i: halo[v, i - 12], 18, 24)
+    sweep(b1, b2, 2, 6, 2, 14)
+    sweep(b2, b1, 4, 4, 4)
+    sweep(b1, b2, 6, 4, 3)
+    rp2[3:7] = restrict(b2)
     boxes2 = [
         (remote(rp2.at[pl.ds(4, 3)], rp2.at[pl.ds(0, 3)], 17, right), has_right),
         (remote(rp2.at[pl.ds(3, 3)], rp2.at[pl.ds(7, 3)], 18, left), has_left),
@@ -354,11 +384,13 @@
     c = coarse_solve(rp2[...], 4 * chip - 3, last_box, inverse[None])
     fixes = unpack(c)
     weight = jnp.full((8, 128), weight_in[core], F32)
+    mine[2].wait()
+    swap[2].wait_recv()
     parts = []
     for i in range(8):
         total = None
         for v in range(5):
-            new = b0[v, 8 + i] + fixes[v][i // 2]
+            new = b2[v, 8 + i] + fixes[v][i // 2]
             b1[v, 8 + i] = new
             term = new * shp[v, i]
             total = term if total is None else total + term
@@ -376,10 +408,10 @@
     me = 2 * cond + core
     shares = []
     for i, (s_to, c_to) in enumerate(ring[1:]):
-        shares.append(remote(cs.at[lax.rem(s_to, 2) * n_cond + c_to], rc.at[me], 19 + i, s_to, c_to))
+        shares.append(remote(cs.at[lax.rem(s_to, 2) * n_cond + c_to], rc.at[me], 21 + i, s_to, c_to))
     for copy in reversed(shares):
         copy.start()
-    back = remote(b1.at[:, pl.ds(8 + 4 * other, 4)], adjoint_out.at[core], 26, sibling)
+    back = remote(b1.at[:, pl.ds(8 + 4 * other, 4)], adjoint_out.at[core], 28, sibling)
     back.start()
     keep = pltpu.make_async_copy(b1.at[:, pl.ds(8 + 4 * core, 4)], adjoint_out.at[core], local_sem.at[0])
     keep.start()
@@ -402,8 +434,7 @@
         def _(copies=copies):
             for copy in copies:
                 copy.wait_send()
-    sent(boxes)
-    sent(boxes2)
+    sent(near_halos + far_halos + boxes + boxes2)
 
 
 def solution(mesh):
@@ -412,29 +443,31 @@
 
     def local(target, shape, jac, sensor, shift, weight, agglomeration, links):
         vmem = lambda *shape: pltpu.VMEM((*shape, 8, 128), F32)
-        hbm = pl.BlockSpec(memory_space=pl.ANY)
-        smem = pl.BlockSpec(memory_space=pltpu.SMEM)
+        hbm = pl.BlockSpec(memory_space=pltpu.HBM)
+        stay = lambda x: pltpu.with_memory_space_constraint(x, pltpu.HBM)
+        operands = (target, shape, jnp.transpose(jac, (1, 2, 0, 3)), sensor, shift, weight)
         return pl.pallas_call(
             functools.partial(kernel, n_cond, n_space),
             out_shape=(
-                jax.ShapeDtypeStruct(target.shape, F32),
-                jax.ShapeDtypeStruct((4, rows, 128), F32),
+                pltpu.VMEM(target.shape, F32),
+                pltpu.VMEM((4, rows, 128), F32),
             ),
-            in_specs=[hbm, hbm, smem, hbm, smem, smem],
-            out_specs=(hbm, pl.BlockSpec(memory_space=pltpu.VMEM)),
+            in_specs=[hbm] * 6,
+            out_specs=(pl.BlockSpec(memory_space=pltpu.VMEM),) * 2,
             scratch_shapes=[
+                pltpu.SMEM((3, 5, 2, 5), F32), pltpu.SMEM((2,), F32), pltpu.SMEM((2,), F32),
                 vmem(5, 20), vmem(22), vmem(5, 8),
                 vmem(21), vmem(4, 20), vmem(20), vmem(20), vmem(75),
-                vmem(5, 24), vmem(5, 24), vmem(5, 12), vmem(5, 4),
+                vmem(5, 24), vmem(5, 24), vmem(5, 24), vmem(5, 12), vmem(5, 4),
                 vmem(18), vmem(10), vmem(2 * n_cond), vmem(2 * n_cond),
-                pltpu.SemaphoreType.DMA((3,)),
+                pltpu.SemaphoreType.DMA((6,)),
                 pltpu.SemaphoreType.DMA((64,)),
-                pltpu.SemaphoreType.DMA((27,)),
+                pltpu.SemaphoreType.DMA((29,)),
             ],
             compiler_params=pltpu.CompilerParams(
                 collective_id=0, has_side_effects=True, vmem_limit_bytes=48 * 2**20
             ),
-        )(target, shape, jac, sensor, shift, weight)
+        )(*map(stay, operands))
 
     in_specs = (
         P("cond", None, "space", None, None),

time: 46.4 us -> 39 us (0.84)
  the two profiles are of different devices: /device:TPU:30 before, /device:TPU:32 now
where the time goes in v2:
time: 39 us; the launch traced here: 38.3 us
  Pallas kernels  36.4 us (93%)
  local copies, waits for them, and re-layouts  1.26 us (3%)
  between operations  0.64 us (2%)
    pallas_call x1, Pallas kernels, local(): pl.pallas_call(functools.partial(kernel, n_cond, n_space), out_shape=(plt...  36.4 us
    unnamed x2, local copies, waits for them, and re-layouts  1.26 us

profile of v2, /device:TPU:32, one launch (start us, length us, event | category | flops | bytes accessed | tf_op | source)
XLA Modules:
  0.0 38.3 jit_solution(17713696784002914325)
XLA Ops:
  0.6 36.4 %shard_map.77 = (f32[2,5,4,8,128]{4,3,2,1,0:T(8,128)S(1)}, f32[4,2,128]{2,1,0:T(2,128)S(1)}) custom-call(f32[2,5,4,8,128]{4,3,2,1,0:T(8,128)} %target_in.1, f32[2,5,4,8,128]{4,3,2,1,0:T(8,128)} %shape_in.1, f32[3,5,2,5]{3,2,1,0:T(2,128)} %bitcast.1, f32[2,4,8,128]{3,2,1,0:T(8,128)} %sensor_in.1, f32[2]{0:T(128)} %shift_hbm.1, f32[2]{0:T(128)} %weight_hbm.1), custom_call_target="tpu_custom_call" | custom-call | tf_op jit(solution)/shard_map/pallas_call | solution.py:449
  37.1 0.7 %copy.10 = f32[2,5,4,8,128]{4,3,2,1,0:T(8,128)} copy(f32[2,5,4,8,128]{4,3,2,1,0:T(8,128)S(1)} %get-tuple-element.2) | data formatting | bytes 327680
  37.8 0.6 %copy.11 = f32[4,2,128]{2,1,0:T(2,128)} copy(f32[4,2,128]{2,1,0:T(2,128)S(1)} %get-tuple-element.3) | data formatting | bytes 8192

commit v3 on v2

--- a/solution.py
+++ b/solution.py
@@ -70,18 +70,30 @@
     )
 
 
+def neighbours(c, first, last_box):
+    own = c[1:-1]
+    at = first + lax.broadcasted_iota(jnp.int32, own.shape, 0)
+    z = lanes(own.shape)
+    total = jnp.where(at == 0, own, c[:-2]) + jnp.where(at == last_box, own, c[2:])
+    total = total + (own + up(own, 4))
+    return total + jnp.where(z < 4, own, behind(own, 4)) + jnp.where(z >= 124, own, ahead(own, 4))
+
+
 def coarse_solve(res, first, last_box, inverse):
-    beta = 8.0 * inverse
     scaled = res * inverse
     c = scaled
     for sweep in range(1, 4):
-        own = c[1:-1]
-        at = first + sweep + lax.broadcasted_iota(jnp.int32, own.shape, 0)
-        z = lanes(own.shape)
-        total = jnp.where(at == 0, own, c[:-2]) + jnp.where(at == last_box, own, c[2:])
-        total = total + (own + up(own, 4))
-        total = total + jnp.where(z < 4, own, behind(own, 4)) + jnp.where(z >= 124, own, ahead(own, 4))
-        c = scaled[sweep:-sweep] + beta * total
+        c = scaled[sweep:-sweep] + 8.0 * inverse * neighbours(c, first + sweep, last_box)
+    return c
+
+
+def coarse_spread(res, first, last_box, inverse):
+    none = jnp.zeros((1, 8, 128), F32)
+    scaled = res * inverse
+    c = scaled
+    for sweep in range(1, 4):
+        scaled = jnp.concatenate([none, scaled, none])
+        c = scaled + 8.0 * inverse * neighbours(jnp.concatenate([none, none, c, none, none]), first - sweep, last_box)
     return c
 
 
@@ -127,7 +139,7 @@
 
 def kernel(
     n_cond, n_space, target_in, shape_in, jac_hbm, sensor_in, shift_hbm, weight_hbm, adjoint_out, sens_out,
-    jac_in, shift_in, weight_in, g, sen, shp, cpx, cyz, w, diag, jac, b0, b1, b2, halo, rs, rp1, rp2, cs, rc, local_sem, send_sem, recv_sem,
+    jac_in, shift_in, weight_in, g, sen, shp, cpx, cyz, w, diag, jac, b0, b1, b2, halo, rs, rp1, rp2, sib, cs, rc, local_sem, send_sem, recv_sem, share_sem, known_sem,
 ):
     space, cond = lax.axis_index("space"), lax.axis_index("cond")
     chip, core = space // 2, space % 2
@@ -136,18 +148,21 @@
     has_left2, has_right2 = chip > 1, chip < chips - 2
     rows = 8 // n_cond
 
+    ring = [(2 * chip + (core + j) % 2, lax.rem(cond + dz, n_cond)) for dz in range(n_cond) for j in range(2)]
+    sibling = 2 * chip + 1 - core
+    following, preceding = lax.rem(cond + 1, n_cond), lax.rem(cond + n_cond - 1, n_cond)
+    beside = [(2 * (chip + near) + j, cond, there) for near, there in ((-1, has_left), (1, has_right)) for j in range(2)]
+    beside += [(sibling, cond, None), (space, following, None), (space, preceding, None)]
+    n_beside = 3 + 2 * (has_left.astype(jnp.int32) + has_right.astype(jnp.int32))
+
+    def tell(semaphore, peers):
+        for s, c, there in peers:
+            def one(s=s, c=c):
+                pl.semaphore_signal(semaphore, inc=1, device_id={"space": s, "cond": c})
+            one() if there is None else pl.when(there)(one)
+
     barrier = pltpu.get_barrier_semaphore()
-    peers = [(2 * chip + 1 - core, cond, None)]
-    for near, there in ((-1, has_left), (1, has_right)):
-        peers += [(2 * (chip + near) + j, cond, there) for j in range(2)]
-    for far, there in ((-2, has_left2), (2, has_right2)):
-        peers.append((2 * (chip + far) + core, cond, there))
-    ring = [(2 * chip + (core + j) % 2, lax.rem(cond + dz, n_cond)) for dz in range(n_cond) for j in range(2)]
-    peers += [(s, c, None) for s, c in ring[2:]]
-    for s, c, there in peers:
-        def greet(s=s, c=c):
-            pl.semaphore_signal(barrier, inc=1, device_id={"space": s, "cond": c})
-        greet() if there is None else pl.when(there)(greet)
+    tell(barrier, beside)
 
     count = iter(range(1000))
     sends = []
@@ -161,7 +176,7 @@
     mine = [
         pltpu.make_async_copy(sensor_in.at[core], sen.at[pl.ds(7 + 4 * core, 4)], local_sem.at[0]),
         pltpu.make_async_copy(target_in.at[core], g.at[:, pl.ds(6 + 4 * core, 4)], local_sem.at[1]),
-        pltpu.make_async_copy(shape_in.at[core], shp.at[:, pl.ds(4 * core, 4)], local_sem.at[2]),
+        pltpu.make_async_copy(shape_in.at[core], shp.at[:, pl.ds(6 + 4 * core, 4)], local_sem.at[2]),
     ]
     small = [
         pltpu.make_async_copy(jac_hbm, jac_in, local_sem.at[3]),
@@ -171,13 +186,56 @@
     for copy in small + mine:
         copy.start()
 
+    pl.semaphore_wait(barrier, n_beside)
+
+    def to_right(k, j):
+        low, size, at = ((2, 2, 0), (0, 4, 2))[k]
+        s_low, s_size, s_at = ((1, 3, 0), (0, 4, 3))[k]
+        there = 2 * (chip + 1) + j
+        return [
+            remote(sensor_in.at[j, pl.ds(s_low, s_size)], sen.at[pl.ds(s_at, s_size)], 3 + 2 * k, there),
+            remote(target_in.at[j, :, pl.ds(low, size)], g.at[:, pl.ds(at, size)], 4 + 2 * k, there),
+            remote(shape_in.at[j, :, pl.ds(low, size)], shp.at[:, pl.ds(at, size)], 21 + k, there),
+        ]
+
+    def to_left(k, j):
+        size, at = ((4, 14), (2, 18))[k]
+        s_size, s_at = ((4, 15), (3, 19))[k]
+        there = 2 * (chip - 1) + j
+        return [
+            remote(sensor_in.at[j, pl.ds(0, s_size)], sen.at[pl.ds(s_at, s_size)], 7 + 2 * k, there),
+            remote(target_in.at[j, :, pl.ds(0, size)], g.at[:, pl.ds(at, size)], 8 + 2 * k, there),
+            remote(shape_in.at[j, :, pl.ds(0, size)], shp.at[:, pl.ds(at, size)], 23 + k, there),
+        ]
+
+    first_round = []
+    for k in range(2):
+        for make, there in ((to_right, has_right), (to_left, has_left)):
+            pairs = [make(k, j) for j in range(2)]
+            first_round.append(([[c[i] for c in pairs] for i in range(3)], jnp.logical_and(there, core == k)))
+    other = 1 - core
+    swap = [
+        remote(sensor_in.at[other], sen.at[pl.ds(7 + 4 * core, 4)], 0, sibling),
+        remote(target_in.at[other], g.at[:, pl.ds(6 + 4 * core, 4)], 1, sibling),
+        remote(shape_in.at[other], shp.at[:, pl.ds(6 + 4 * core, 4)], 2, sibling),
+    ]
+    for copies, there in first_round:
+        @pl.when(there)
+        def _(copies=copies):
+            for copy in copies[0] + copies[1]:
+                copy.start()
+    for copy in swap[:2]:
+        copy.start()
+    tell(known_sem.at[0], beside)
+
     @pl.when(jnp.logical_not(has_left))
     def _():
         g[:, 0:6] = jnp.zeros((5, 6, 8, 128), F32)
         sen[0:7] = jnp.zeros((7, 8, 128), F32)
         halo[:, 0:6] = jnp.zeros((5, 6, 8, 128), F32)
         rp1[3:7] = jnp.zeros((4, 8, 128), F32)
-        rp2[0:3] = jnp.zeros((3, 8, 128), F32)
+        rp2[:, 0:3] = jnp.zeros((2, 3, 8, 128), F32)
+        rc[0] = jnp.zeros(rc.shape[1:], F32)
 
     @pl.when(jnp.logical_not(has_right))
     def _():
@@ -185,7 +243,8 @@
         sen[15:22] = jnp.zeros((7, 8, 128), F32)
         halo[:, 6:12] = jnp.zeros((5, 6, 8, 128), F32)
         rp1[11:15] = jnp.zeros((4, 8, 128), F32)
-        rp2[7:10] = jnp.zeros((3, 8, 128), F32)
+        rp2[:, 7:10] = jnp.zeros((2, 3, 8, 128), F32)
+        rc[2] = jnp.zeros(rc.shape[1:], F32)
 
     @pl.when(jnp.logical_not(has_left2))
     def _():
@@ -203,51 +262,6 @@
                 jac[d * 25 + u * 5 + v] = jnp.full((8, 128), 0.5 * jac_in[d, u, core, v], F32)
     shift = jnp.full((8, 128), shift_in[core], F32)
     inverse = 1.0 / (shift * 32.0 + 48.0)
-
-    n_peers = 1 + 2 * (n_cond - 1)
-    pl.semaphore_wait(
-        barrier,
-        n_peers + 2 * has_left.astype(jnp.int32) + 2 * has_right.astype(jnp.int32)
-        + has_left2.astype(jnp.int32) + has_right2.astype(jnp.int32),
-    )
-
-    def to_right(k, j):
-        low, size, at = ((2, 2, 0), (0, 4, 2))[k]
-        s_low, s_size, s_at = ((1, 3, 0), (0, 4, 3))[k]
-        there = 2 * (chip + 1) + j
-        return [
-            remote(sensor_in.at[j, pl.ds(s_low, s_size)], sen.at[pl.ds(s_at, s_size)], 3 + 2 * k, there),
-            remote(target_in.at[j, :, pl.ds(low, size)], g.at[:, pl.ds(at, size)], 4 + 2 * k, there),
-        ]
-
-    def to_left(k, j):
-        size, at = ((4, 14), (2, 18))[k]
-        s_size, s_at = ((4, 15), (3, 19))[k]
-        there = 2 * (chip - 1) + j
-        return [
-            remote(sensor_in.at[j, pl.ds(0, s_size)], sen.at[pl.ds(s_at, s_size)], 7 + 2 * k, there),
-            remote(target_in.at[j, :, pl.ds(0, size)], g.at[:, pl.ds(at, size)], 8 + 2 * k, there),
-        ]
-
-    first_round = []
-    for k in range(2):
-        for make, there in ((to_right, has_right), (to_left, has_left)):
-            pairs = [make(k, j) for j in range(2)]
-            first_round.append(([c[0] for c in pairs] + [c[1] for c in pairs], jnp.logical_and(there, core == k)))
-    other = 1 - core
-    sibling = 2 * chip + other
-    swap = [
-        remote(sensor_in.at[other], sen.at[pl.ds(7 + 4 * core, 4)], 0, sibling),
-        remote(target_in.at[other], g.at[:, pl.ds(6 + 4 * core, 4)], 1, sibling),
-        remote(shape_in.at[other], shp.at[:, pl.ds(4 * core, 4)], 2, sibling),
-    ]
-    for copies, there in first_round:
-        @pl.when(there)
-        def _(copies=copies):
-            for copy in copies:
-                copy.start()
-    for copy in swap:
-        copy.start()
 
     awaited = [(make(k, 0), there) for k in range(2) for make, there in ((to_right, has_left), (to_left, has_right))]
 
@@ -286,7 +300,6 @@
     cpx[0:1] = (sen[0:1] + sen[1:2]) * 0.25 + 4.0 * EPS
     lax.fori_loop(0, 5, coefficients, 0)
     arrive_first(1)
-
     def begin(k, carry):
         i = 4 * k
         weight = w[pl.ds(i, 4)]
@@ -337,6 +350,8 @@
 
     sweep(b0, b1, 4, 4, 4)
     sweep(b1, b0, 6, 4, 3)
+    pl.semaphore_wait(known_sem.at[0], n_beside)
+    tell(known_sem.at[1], [(space, preceding, None)])
     near_halos = [
         (remote(b0.at[:, pl.ds(12, 2)], halo.at[:, pl.ds(4, 2)], 11, right), has_right),
         (remote(b0.at[:, pl.ds(10, 2)], halo.at[:, pl.ds(6, 2)], 12, left), has_left),
@@ -355,6 +370,13 @@
     ]
     start(boxes)
     start(far_halos)
+    swap[2].start()
+    for copies, there in first_round:
+        @pl.when(there)
+        def _(copies=copies):
+            for copy in copies[2]:
+                copy.start()
+
     arrive(boxes, (has_left2, has_right2, has_left, has_right))
     last_box = 4 * chips - 1
     c = coarse_solve(rp1[...], 4 * chip - 7, last_box, inverse[None])
@@ -374,65 +396,108 @@
     sweep(b1, b2, 2, 6, 2, 14)
     sweep(b2, b1, 4, 4, 4)
     sweep(b1, b2, 6, 4, 3)
-    rp2[3:7] = restrict(b2)
-    boxes2 = [
-        (remote(rp2.at[pl.ds(4, 3)], rp2.at[pl.ds(0, 3)], 17, right), has_right),
-        (remote(rp2.at[pl.ds(3, 3)], rp2.at[pl.ds(7, 3)], 18, left), has_left),
-    ]
+    over = remote(b2.at[:, pl.ds(8 + 4 * other, 4)], sib, 25, sibling)
+    over.start()
+    rp2[core, 3:7] = restrict(b2)
+
+    def boxes_beside(c_at, j):
+        return [
+            (remote(rp2.at[c_at, pl.ds(4, 3)], rp2.at[c_at, pl.ds(0, 3)], 17 + 9 * c_at, right - core + j), has_right),
+            (remote(rp2.at[c_at, pl.ds(3, 3)], rp2.at[c_at, pl.ds(7, 3)], 18 + 9 * c_at, left - core + j), has_left),
+        ]
+
+    boxes2 = boxes_beside(core, 0) + boxes_beside(core, 1)
     start(boxes2)
-    arrive(boxes2, (has_left, has_right))
-    c = coarse_solve(rp2[...], 4 * chip - 3, last_box, inverse[None])
-    fixes = unpack(c)
+    boxes_over = remote(rp2.at[core, pl.ds(3, 4)], rp2.at[core, pl.ds(3, 4)], 28, sibling)
+    boxes_over.start()
+
     weight = jnp.full((8, 128), weight_in[core], F32)
     mine[2].wait()
     swap[2].wait_recv()
+    for copies, there in awaited:
+        pl.when(there)(copies[2].wait_recv)
+    fixes = unpack(coarse_spread(rp2[core, 3:7], 4 * chip, last_box, inverse[None]))
     parts = []
-    for i in range(8):
+    for i in range(20):
         total = None
         for v in range(5):
-            new = b2[v, 8 + i] + fixes[v][i // 2]
-            b1[v, 8 + i] = new
-            term = new * shp[v, i]
+            value = fixes[v][i // 2]
+            if 6 <= i < 14:
+                value = value + b2[v, 2 + i]
+            term = value * shp[v, i]
             total = term if total is None else total + term
         parts.append(weight * total)
-
     s2 = sublanes((8, 128))
-    for j in range(2):
-        for c_to in range(n_cond):
-            gathered = None
+    for d in range(3):
+        for j in range(2):
+            for c_to in range(n_cond):
+                gathered = jnp.zeros((8, 128), F32)
+                for i in range(4):
+                    at = 8 * d - 2 + 4 * j + i
+                    turn = (rows * i - rows * c_to) % 8
+                    moved = jnp.zeros((8, 128), F32)
+                    if 0 <= at < 20:
+                        moved = parts[at] if turn == 0 else down(parts[at], turn)
+                    gathered = jnp.where(s2 >= rows * i, moved, gathered) if i else moved
+                cs[d, j * n_cond + c_to] = gathered
+    me = 2 * cond + core
+
+    def share(d, j, c_to):
+        return pltpu.make_async_remote_copy(
+            src_ref=cs.at[d, j * n_cond + c_to], dst_ref=rc.at[2 - d, me], send_sem=share_sem.at[d], recv_sem=share_sem.at[5 - d],
+            device_id={"space": 2 * (chip + d - 1) + j, "cond": c_to},
+        )
+
+    def shared(d, slots):
+        return pltpu.make_async_remote_copy(
+            src_ref=cs.at[d, pl.ds(0, slots)], dst_ref=rc.at[d, pl.ds(0, slots)], send_sem=share_sem.at[d], recv_sem=share_sem.at[3 + d],
+            device_id={"space": sibling, "cond": cond},
+        )
+
+    pl.semaphore_wait(known_sem.at[1], 1)
+    outer = ((0, has_left), (2, has_right))
+    for dz in (2, 1, 3, 0):
+        for d, there in outer:
+            @pl.when(there)
+            def _(d=d, dz=dz):
+                for j in range(2):
+                    share(d, j, lax.rem(cond + dz, n_cond)).start()
+    for s_to, c_to in reversed(ring[1:]):
+        share(1, lax.rem(s_to, 2), c_to).start()
+    rc[1, me] = cs[1, core * n_cond + cond]
+
+    arrive(boxes_beside(0, 0) + boxes_beside(1, 0), (has_left, has_right) * 2)
+    boxes_over.wait_recv()
+    over.wait_recv()
+    for c_at, old in ((core, lambda v: b2[v, pl.ds(8 + 4 * core, 4)]), (other, lambda v: sib[v])):
+        inv = 1.0 / (jnp.full((1, 8, 128), shift_in[c_at], F32) * 32.0 + 48.0)
+        c = coarse_solve(rp2[c_at, pl.ds(2 * core, 8)], 4 * chip - 3 + 2 * core, last_box, inv)
+        fixes = unpack(c)
+        for v in range(5):
+            value = old(v)
             for i in range(4):
-                turn = (rows * i - rows * c_to) % 8
-                moved = parts[4 * j + i] if turn == 0 else down(parts[4 * j + i], turn)
-                gathered = moved if gathered is None else jnp.where(s2 >= rows * i, moved, gathered)
-            cs[j * n_cond + c_to] = gathered
-    me = 2 * cond + core
-    shares = []
-    for i, (s_to, c_to) in enumerate(ring[1:]):
-        shares.append(remote(cs.at[lax.rem(s_to, 2) * n_cond + c_to], rc.at[me], 21 + i, s_to, c_to))
-    for copy in reversed(shares):
-        copy.start()
-    back = remote(b1.at[:, pl.ds(8 + 4 * other, 4)], adjoint_out.at[core], 28, sibling)
-    back.start()
-    keep = pltpu.make_async_copy(b1.at[:, pl.ds(8 + 4 * core, 4)], adjoint_out.at[core], local_sem.at[0])
-    keep.start()
-    rc[me] = cs[core * n_cond + cond]
-    for copy in shares:
-        copy.wait_recv()
-    total = rc[0]
-    for i in range(1, 2 * n_cond):
-        total = total + rc[i]
+                adjoint_out[c_at, v, i] = value[i] + fixes[v][i // 2]
+
+    for d, there in outer:
+        pl.when(there)(shared(d, 2 * n_cond).wait_recv)
+    shared(1, 2 * n_cond - 1).wait_recv()
+    total = None
+    for d in range(3):
+        for i in range(2 * n_cond):
+            total = rc[d, i] if total is None else total + rc[d, i]
     for i in range(4):
         sens_out[i] = total[rows * i : rows * (i + 1)]
-    keep.wait()
-    back.wait()
-    for copy in shares:
-        copy.wait_send()
+    over.wait_send()
+    boxes_over.wait_send()
+    for d, there in outer:
+        pl.when(there)(shared(d, 2 * n_cond).wait_send)
+    shared(1, 2 * n_cond - 1).wait_send()
     for copy in swap:
         copy.wait_send()
     for copies, there in first_round:
         @pl.when(there)
         def _(copies=copies):
-            for copy in copies:
+            for copy in copies[0] + copies[1] + copies[2]:
                 copy.wait_send()
     sent(near_halos + far_halos + boxes + boxes2)
 
@@ -456,13 +521,15 @@
             out_specs=(pl.BlockSpec(memory_space=pltpu.VMEM),) * 2,
             scratch_shapes=[
                 pltpu.SMEM((3, 5, 2, 5), F32), pltpu.SMEM((2,), F32), pltpu.SMEM((2,), F32),
-                vmem(5, 20), vmem(22), vmem(5, 8),
+                vmem(5, 20), vmem(22), vmem(5, 20),
                 vmem(21), vmem(4, 20), vmem(20), vmem(20), vmem(75),
                 vmem(5, 24), vmem(5, 24), vmem(5, 24), vmem(5, 12), vmem(5, 4),
-                vmem(18), vmem(10), vmem(2 * n_cond), vmem(2 * n_cond),
+                vmem(18), vmem(2, 10), vmem(5, 4), vmem(3, 2 * n_cond), vmem(3, 2 * n_cond),
                 pltpu.SemaphoreType.DMA((6,)),
                 pltpu.SemaphoreType.DMA((64,)),
                 pltpu.SemaphoreType.DMA((29,)),
+                pltpu.SemaphoreType.DMA((6,)),
+                pltpu.SemaphoreType.REGULAR((2,)),
             ],
             compiler_params=pltpu.CompilerParams(
                 collective_id=0, has_side_effects=True, vmem_limit_bytes=48 * 2**20

time: 39 us -> 36.8 us (0.944); the launches traced: 38.3 us -> 36.7 us
  Pallas kernels: 36.4 us -> 34.8 us
    pallas_call x1, Pallas kernels: 36.4 us -> 34.8 us  [local(): pl.pallas_call(functools.partial(kernel, n_cond, n_space), out_shape=(plt...]
where the time goes in v3:
time: 36.8 us; the launch traced here: 36.7 us
  Pallas kernels  34.8 us (95%)
  local copies, waits for them, and re-layouts  1.26 us (3%)
  between operations  0.64 us (2%)
    pallas_call x1, Pallas kernels, local(): pl.pallas_call(functools.partial(kernel, n_cond, n_space), out_shape=(plt...  34.8 us
    unnamed x2, local copies, waits for them, and re-layouts  1.26 us

profile of v3, /device:TPU:32, one launch (start us, length us, event | category | flops | bytes accessed | tf_op | source)
XLA Modules:
  0.0 36.7 jit_solution(8957154122409451780)
XLA Ops:
  0.6 34.8 %shard_map.77 = (f32[2,5,4,8,128]{4,3,2,1,0:T(8,128)S(1)}, f32[4,2,128]{2,1,0:T(2,128)S(1)}) custom-call(f32[2,5,4,8,128]{4,3,2,1,0:T(8,128)} %target_in.1, f32[2,5,4,8,128]{4,3,2,1,0:T(8,128)} %shape_in.1, f32[3,5,2,5]{3,2,1,0:T(2,128)} %bitcast.1, f32[2,4,8,128]{3,2,1,0:T(8,128)} %sensor_in.1, f32[2]{0:T(128)} %shift_hbm.1, f32[2]{0:T(128)} %weight_hbm.1), custom_call_target="tpu_custom_call" | custom-call | tf_op jit(solution)/shard_map/pallas_call | solution.py:514
  35.4 0.7 %copy.10 = f32[2,5,4,8,128]{4,3,2,1,0:T(8,128)} copy(f32[2,5,4,8,128]{4,3,2,1,0:T(8,128)S(1)} %get-tuple-element.2) | data formatting | bytes 327680
  36.1 0.6 %copy.11 = f32[4,2,128]{2,1,0:T(2,128)} copy(f32[4,2,128]{2,1,0:T(2,128)S(1)} %get-tuple-element.3) | data formatting | bytes 8192

commit v4 on v3

--- a/solution.py
+++ b/solution.py
@@ -209,8 +209,8 @@
         ]
 
     first_round = []
-    for k in range(2):
-        for make, there in ((to_right, has_right), (to_left, has_left)):
+    for near in (True, False):
+        for make, there, k in ((to_right, has_right, 1 if near else 0), (to_left, has_left, 0 if near else 1)):
             pairs = [make(k, j) for j in range(2)]
             first_round.append(([[c[i] for c in pairs] for i in range(3)], jnp.logical_and(there, core == k)))
     other = 1 - core
@@ -219,13 +219,17 @@
         remote(target_in.at[other], g.at[:, pl.ds(6 + 4 * core, 4)], 1, sibling),
         remote(shape_in.at[other], shp.at[:, pl.ds(6 + 4 * core, 4)], 2, sibling),
     ]
-    for copies, there in first_round:
-        @pl.when(there)
-        def _(copies=copies):
-            for copy in copies[0] + copies[1]:
-                copy.start()
+    def send_first(items):
+        for copies, there in items:
+            @pl.when(there)
+            def _(copies=copies):
+                for copy in copies[0] + copies[1]:
+                    copy.start()
+
+    send_first(first_round[:2])
     for copy in swap[:2]:
         copy.start()
+    send_first(first_round[2:])
     tell(known_sem.at[0], beside)
 
     @pl.when(jnp.logical_not(has_left))
@@ -263,15 +267,17 @@
     shift = jnp.full((8, 128), shift_in[core], F32)
     inverse = 1.0 / (shift * 32.0 + 48.0)
 
-    awaited = [(make(k, 0), there) for k in range(2) for make, there in ((to_right, has_left), (to_left, has_right))]
-
-    def arrive_first(i):
-        mine[i].wait()
-        swap[i].wait_recv()
-        for copies, there in awaited:
-            pl.when(there)(copies[i].wait_recv)
-
-    arrive_first(0)
+    from_left, from_right = ([make(k, 0) for k in range(2)] for make in (to_right, to_left))
+
+    def arrive_first(i, copies, there):
+        @pl.when(there)
+        def _():
+            for copy in copies:
+                copy[i].wait_recv()
+
+    mine[0].wait()
+    swap[0].wait_recv()
+    arrive_first(0, from_left, has_left)
 
     s, z = sublanes((1, 8, 128)), lanes((1, 8, 128))
 
@@ -298,16 +304,14 @@
 
     low_layer, high_layer = jnp.where(has_left, 0, 6), jnp.where(has_right, 20, 14)
     cpx[0:1] = (sen[0:1] + sen[1:2]) * 0.25 + 4.0 * EPS
-    lax.fori_loop(0, 5, coefficients, 0)
-    arrive_first(1)
+    lax.fori_loop(0, 3, coefficients, 0)
+
     def begin(k, carry):
         i = 4 * k
         weight = w[pl.ds(i, 4)]
         for v in range(5):
             b0[v, pl.ds(i + 2, 4)] = weight * g[v, pl.ds(i, 4)]
         return carry
-
-    lax.fori_loop(0, 5, begin, 0)
 
     def sweep(src, dst, low, n, times, stride=None):
         def body(i, carry):
@@ -348,25 +352,35 @@
         for copy, there in copies:
             pl.when(there)(copy.wait_send)
 
-    sweep(b0, b1, 4, 4, 4)
-    sweep(b1, b0, 6, 4, 3)
+    mine[1].wait()
+    swap[1].wait_recv()
+    arrive_first(1, from_left, has_left)
+    lax.fori_loop(0, 3, begin, 0)
+    sweep(b0, b1, 4, 4, 2)
+    sweep(b1, b2, 6, 4, 1)
+    arrive_first(0, from_right, has_right)
+    lax.fori_loop(3, 5, coefficients, 0)
+    arrive_first(1, from_right, has_right)
+    lax.fori_loop(3, 5, begin, 0)
+    sweep(b0, b1, 12, 4, 2)
+    sweep(b1, b2, 10, 4, 2)
     pl.semaphore_wait(known_sem.at[0], n_beside)
     tell(known_sem.at[1], [(space, preceding, None)])
     near_halos = [
-        (remote(b0.at[:, pl.ds(12, 2)], halo.at[:, pl.ds(4, 2)], 11, right), has_right),
-        (remote(b0.at[:, pl.ds(10, 2)], halo.at[:, pl.ds(6, 2)], 12, left), has_left),
+        (remote(b2.at[:, pl.ds(12, 2)], halo.at[:, pl.ds(4, 2)], 11, right), has_right),
+        (remote(b2.at[:, pl.ds(10, 2)], halo.at[:, pl.ds(6, 2)], 12, left), has_left),
     ]
     far_halos = [
-        (remote(b0.at[:, pl.ds(8, 4)], halo.at[:, pl.ds(0, 4)], 19, right), has_right),
-        (remote(b0.at[:, pl.ds(12, 4)], halo.at[:, pl.ds(8, 4)], 20, left), has_left),
+        (remote(b2.at[:, pl.ds(8, 4)], halo.at[:, pl.ds(0, 4)], 19, right), has_right),
+        (remote(b2.at[:, pl.ds(12, 4)], halo.at[:, pl.ds(8, 4)], 20, left), has_left),
     ]
     start(near_halos)
-    rp1[7:11] = restrict(b0)
+    rp1[7:11] = restrict(b2)
     boxes = [
+        (remote(rp1.at[pl.ds(7, 4)], rp1.at[pl.ds(3, 4)], 15, right), has_right),
+        (remote(rp1.at[pl.ds(7, 4)], rp1.at[pl.ds(11, 4)], 16, left), has_left),
         (remote(rp1.at[pl.ds(8, 3)], rp1.at[pl.ds(0, 3)], 13, space + 4), has_right2),
         (remote(rp1.at[pl.ds(7, 3)], rp1.at[pl.ds(15, 3)], 14, space - 4), has_left2),
-        (remote(rp1.at[pl.ds(7, 4)], rp1.at[pl.ds(3, 4)], 15, right), has_right),
-        (remote(rp1.at[pl.ds(7, 4)], rp1.at[pl.ds(11, 4)], 16, left), has_left),
     ]
     start(boxes)
     start(far_halos)
@@ -377,7 +391,7 @@
             for copy in copies[2]:
                 copy.start()
 
-    arrive(boxes, (has_left2, has_right2, has_left, has_right))
+    arrive(boxes, (has_left, has_right, has_left2, has_right2))
     last_box = 4 * chips - 1
     c = coarse_solve(rp1[...], 4 * chip - 7, last_box, inverse[None])
     at = 4 * chip - 4 + lax.broadcasted_iota(jnp.int32, c.shape, 0)
@@ -388,17 +402,17 @@
             for i in range(low, high):
                 b1[v, i] = old(v, i) + fixes[v][i // 2]
 
-    correct(lambda v, i: b0[v, i], 6, 18)
-    sweep(b1, b2, 8, 4, 2)
+    correct(lambda v, i: b2[v, i], 6, 18)
+    sweep(b1, b0, 8, 4, 2)
     arrive(near_halos + far_halos, (has_left, has_right) * 2)
     correct(lambda v, i: halo[v, i], 0, 6)
     correct(lambda v, i: halo[v, i - 12], 18, 24)
-    sweep(b1, b2, 2, 6, 2, 14)
-    sweep(b2, b1, 4, 4, 4)
-    sweep(b1, b2, 6, 4, 3)
-    over = remote(b2.at[:, pl.ds(8 + 4 * other, 4)], sib, 25, sibling)
+    sweep(b1, b0, 2, 6, 2, 14)
+    sweep(b0, b1, 4, 4, 4)
+    sweep(b1, b0, 6, 4, 3)
+    over = remote(b0.at[:, pl.ds(8 + 4 * other, 4)], sib, 25, sibling)
     over.start()
-    rp2[core, 3:7] = restrict(b2)
+    rp2[core, 3:7] = restrict(b0)
 
     def boxes_beside(c_at, j):
         return [
@@ -407,15 +421,12 @@
         ]
 
     boxes2 = boxes_beside(core, 0) + boxes_beside(core, 1)
-    start(boxes2)
-    boxes_over = remote(rp2.at[core, pl.ds(3, 4)], rp2.at[core, pl.ds(3, 4)], 28, sibling)
-    boxes_over.start()
 
     weight = jnp.full((8, 128), weight_in[core], F32)
     mine[2].wait()
     swap[2].wait_recv()
-    for copies, there in awaited:
-        pl.when(there)(copies[2].wait_recv)
+    arrive_first(2, from_left, has_left)
+    arrive_first(2, from_right, has_right)
     fixes = unpack(coarse_spread(rp2[core, 3:7], 4 * chip, last_box, inverse[None]))
     parts = []
     for i in range(20):
@@ -423,7 +434,7 @@
         for v in range(5):
             value = fixes[v][i // 2]
             if 6 <= i < 14:
-                value = value + b2[v, 2 + i]
+                value = value + b0[v, 2 + i]
             term = value * shp[v, i]
             total = term if total is None else total + term
         parts.append(weight * total)
@@ -466,10 +477,14 @@
         share(1, lax.rem(s_to, 2), c_to).start()
     rc[1, me] = cs[1, core * n_cond + cond]
 
+    start(boxes2)
+    boxes_over = remote(rp2.at[core, pl.ds(3, 4)], rp2.at[core, pl.ds(3, 4)], 28, sibling)
+    boxes_over.start()
+
     arrive(boxes_beside(0, 0) + boxes_beside(1, 0), (has_left, has_right) * 2)
     boxes_over.wait_recv()
     over.wait_recv()
-    for c_at, old in ((core, lambda v: b2[v, pl.ds(8 + 4 * core, 4)]), (other, lambda v: sib[v])):
+    for c_at, old in ((core, lambda v: b0[v, pl.ds(8 + 4 * core, 4)]), (other, lambda v: sib[v])):
         inv = 1.0 / (jnp.full((1, 8, 128), shift_in[c_at], F32) * 32.0 + 48.0)
         c = coarse_solve(rp2[c_at, pl.ds(2 * core, 8)], 4 * chip - 3 + 2 * core, last_box, inv)
         fixes = unpack(c)
@@ -502,6 +517,14 @@
     sent(near_halos + far_halos + boxes + boxes2)
 
 
+def settle(adjoint, sens, adjoint_out, sens_out, sem):
+    copies = [pltpu.make_async_copy(adjoint, adjoint_out, sem.at[0]), pltpu.make_async_copy(sens, sens_out, sem.at[1])]
+    for copy in copies:
+        copy.start()
+    for copy in copies:
+        copy.wait()
+
+
 def solution(mesh):
     n_cond, n_space = mesh.shape["cond"], mesh.shape["space"]
     rows = 8 // n_cond
@@ -511,7 +534,7 @@
         hbm = pl.BlockSpec(memory_space=pltpu.HBM)
         stay = lambda x: pltpu.with_memory_space_constraint(x, pltpu.HBM)
         operands = (target, shape, jnp.transpose(jac, (1, 2, 0, 3)), sensor, shift, weight)
-        return pl.pallas_call(
+        adjoint, sens = pl.pallas_call(
             functools.partial(kernel, n_cond, n_space),
             out_shape=(
                 pltpu.VMEM(target.shape, F32),
@@ -535,6 +558,13 @@
                 collective_id=0, has_side_effects=True, vmem_limit_bytes=48 * 2**20
             ),
         )(*map(stay, operands))
+        return pl.pallas_call(
+            settle,
+            out_shape=(pltpu.HBM(adjoint.shape, F32), pltpu.HBM(sens.shape, F32)),
+            in_specs=[pl.BlockSpec(memory_space=pltpu.VMEM)] * 2,
+            out_specs=(hbm, hbm),
+            scratch_shapes=[pltpu.SemaphoreType.DMA((2,))],
+        )(*(pltpu.with_memory_space_constraint(x, pltpu.VMEM) for x in (adjoint, sens)))
 
     in_specs = (
         P("cond", None, "space", None, None),

time: 36.8 us -> 35.9 us (0.976)
  local copies, waits for them, and re-layouts: 1.26 us -> 0 us
    unnamed x2 -> x0, local copies, waits for them, and re-layouts: 1.26 us -> none
    pallas_call x0 -> x1, Pallas kernels: none -> 0.69 us  [local(): pl.pallas_call(settle, out_shape=(pltpu.HBM(adjoint.shape, F32), pltpu.HB...]
    pallas_call x1, Pallas kernels: 34.8 us -> 34.4 us  [local(): pl.pallas_call(functools.partial(kernel, n_cond, n_space), out_shape=(plt...]
where the time goes in v4:
time: 35.9 us; the launch traced here: 35.7 us
  Pallas kernels  35.1 us (98%)
  between operations  0.64 us (2%)
    pallas_call x1, Pallas kernels, local(): pl.pallas_call(functools.partial(kernel, n_cond, n_space), out_shape=(plt...  34.4 us

profile of v4, /device:TPU:32, one launch (start us, length us, event | category | flops | bytes accessed | tf_op | source)
XLA Modules:
  0.0 35.7 jit_solution(10264829810609662209)
XLA Ops:
  0.6 34.4 %shard_map.77 = (f32[2,5,4,8,128]{4,3,2,1,0:T(8,128)S(1)}, f32[4,2,128]{2,1,0:T(2,128)S(1)}) custom-call(f32[2,5,4,8,128]{4,3,2,1,0:T(8,128)} %target_in.1, f32[2,5,4,8,128]{4,3,2,1,0:T(8,128)} %shape_in.1, f32[3,5,2,5]{3,2,1,0:T(2,128)} %bitcast.1, f32[2,4,8,128]{3,2,1,0:T(8,128)} %sensor_in.1, f32[2]{0:T(128)} %shift_hbm.1, f32[2]{0:T(128)} %weight_hbm.1), custom_call_target="tpu_custom_call" | custom-call | tf_op jit(solution)/shard_map/pallas_call | solution.py:537
  35.0 0.7 %shard_map.78 = (f32[2,5,4,8,128]{4,3,2,1,0:T(8,128)}, f32[4,2,128]{2,1,0:T(2,128)}) custom-call(f32[2,5,4,8,128]{4,3,2,1,0:T(8,128)S(1)} %get-tuple-element.4.adjoint, f32[4,2,128]{2,1,0:T(2,128)S(1)} %get-tuple-element.5.sens), custom_call_target="tpu_custom_call" | custom-call | tf_op jit(solution)/shard_map/pallas_call | solution.py:561

commit v5 on v4

--- a/solution.py
+++ b/solution.py
@@ -230,6 +230,13 @@
     for copy in swap[:2]:
         copy.start()
     send_first(first_round[2:])
+    swap[2].start()
+    for copies, there in first_round:
+        @pl.when(there)
+        def _(copies=copies):
+            for copy in copies[2]:
+                copy.start()
+
     tell(known_sem.at[0], beside)
 
     @pl.when(jnp.logical_not(has_left))
@@ -306,6 +313,20 @@
     cpx[0:1] = (sen[0:1] + sen[1:2]) * 0.25 + 4.0 * EPS
     lax.fori_loop(0, 3, coefficients, 0)
 
+    right, left = space + 2, space - 2
+
+    def start(copies):
+        for copy, there in copies:
+            pl.when(there)(copy.start)
+
+    def arrive(copies, theres):
+        for (copy, _), there in zip(copies, theres):
+            pl.when(there)(copy.wait_recv)
+
+    def sent(copies):
+        for copy, there in copies:
+            pl.when(there)(copy.wait_send)
+
     def begin(k, carry):
         i = 4 * k
         weight = w[pl.ds(i, 4)]
@@ -314,12 +335,20 @@
         return carry
 
     def sweep(src, dst, low, n, times, stride=None):
+        part = 2
+
         def body(i, carry):
-            at = low + i * (stride or n)
-            center, out = off_diagonal(src, at, n, jac, cpx, cyz)
-            weight = w[pl.ds(at - 2, n)]
-            for v in range(5):
-                dst[v, pl.ds(at, n)] = (1.0 - RELAX) * center[v] + weight * (g[v, pl.ds(at - 2, n)] + out[v])
+            results = []
+            for k in range(n // part):
+                at = low + i * (stride or n) + k * part
+                center, out = off_diagonal(src, at, part, jac, cpx, cyz)
+                weight = w[pl.ds(at - 2, part)]
+                results.append([
+                    (1.0 - RELAX) * center[v] + weight * (g[v, pl.ds(at - 2, part)] + out[v]) for v in range(5)
+                ])
+            for k, values in enumerate(results):
+                for v in range(5):
+                    dst[v, pl.ds(low + i * (stride or n) + k * part, part)] = values[v]
             return carry
 
         lax.fori_loop(0, times, body, 0)
@@ -338,32 +367,20 @@
         lax.fori_loop(0, 2, body, 0)
         return pack([rs[v] for v in range(5)])
 
-    right, left = space + 2, space - 2
-
-    def start(copies):
-        for copy, there in copies:
-            pl.when(there)(copy.start)
-
-    def arrive(copies, theres):
-        for (copy, _), there in zip(copies, theres):
-            pl.when(there)(copy.wait_recv)
-
-    def sent(copies):
-        for copy, there in copies:
-            pl.when(there)(copy.wait_send)
-
     mine[1].wait()
     swap[1].wait_recv()
     arrive_first(1, from_left, has_left)
     lax.fori_loop(0, 3, begin, 0)
-    sweep(b0, b1, 4, 4, 2)
+    sweep(b0, b1, 4, 8, 1)
     sweep(b1, b2, 6, 4, 1)
+    early_halo = [(remote(b2.at[:, pl.ds(8, 2)], halo.at[:, pl.ds(0, 2)], 29, right), has_right)]
+    start(early_halo)
     arrive_first(0, from_right, has_right)
     lax.fori_loop(3, 5, coefficients, 0)
     arrive_first(1, from_right, has_right)
     lax.fori_loop(3, 5, begin, 0)
-    sweep(b0, b1, 12, 4, 2)
-    sweep(b1, b2, 10, 4, 2)
+    sweep(b0, b1, 12, 8, 1)
+    sweep(b1, b2, 10, 8, 1)
     pl.semaphore_wait(known_sem.at[0], n_beside)
     tell(known_sem.at[1], [(space, preceding, None)])
     near_halos = [
@@ -371,7 +388,7 @@
         (remote(b2.at[:, pl.ds(10, 2)], halo.at[:, pl.ds(6, 2)], 12, left), has_left),
     ]
     far_halos = [
-        (remote(b2.at[:, pl.ds(8, 4)], halo.at[:, pl.ds(0, 4)], 19, right), has_right),
+        (remote(b2.at[:, pl.ds(10, 2)], halo.at[:, pl.ds(2, 2)], 19, right), has_right),
         (remote(b2.at[:, pl.ds(12, 4)], halo.at[:, pl.ds(8, 4)], 20, left), has_left),
     ]
     start(near_halos)
@@ -384,13 +401,6 @@
     ]
     start(boxes)
     start(far_halos)
-    swap[2].start()
-    for copies, there in first_round:
-        @pl.when(there)
-        def _(copies=copies):
-            for copy in copies[2]:
-                copy.start()
-
     arrive(boxes, (has_left, has_right, has_left2, has_right2))
     last_box = 4 * chips - 1
     c = coarse_solve(rp1[...], 4 * chip - 7, last_box, inverse[None])
@@ -402,14 +412,18 @@
             for i in range(low, high):
                 b1[v, i] = old(v, i) + fixes[v][i // 2]
 
+    arrive(near_halos, (has_left, has_right))
+    correct(lambda v, i: halo[v, i], 4, 6)
     correct(lambda v, i: b2[v, i], 6, 18)
-    sweep(b1, b0, 8, 4, 2)
-    arrive(near_halos + far_halos, (has_left, has_right) * 2)
-    correct(lambda v, i: halo[v, i], 0, 6)
-    correct(lambda v, i: halo[v, i - 12], 18, 24)
-    sweep(b1, b0, 2, 6, 2, 14)
-    sweep(b0, b1, 4, 4, 4)
-    sweep(b1, b0, 6, 4, 3)
+    correct(lambda v, i: halo[v, i - 12], 18, 20)
+    sweep(b1, b0, 6, 6, 2)
+    sweep(b0, b1, 8, 8, 1)
+    arrive(early_halo + far_halos, (has_left, has_left, has_right))
+    correct(lambda v, i: halo[v, i], 0, 4)
+    correct(lambda v, i: halo[v, i - 12], 20, 24)
+    sweep(b1, b0, 2, 4, 2, 16)
+    sweep(b0, b1, 4, 4, 2, 12)
+    sweep(b1, b0, 6, 6, 2)
     over = remote(b0.at[:, pl.ds(8 + 4 * other, 4)], sib, 25, sibling)
     over.start()
     rp2[core, 3:7] = restrict(b0)
@@ -514,7 +528,7 @@
         def _(copies=copies):
             for copy in copies[0] + copies[1] + copies[2]:
                 copy.wait_send()
-    sent(near_halos + far_halos + boxes + boxes2)
+    sent(early_halo + near_halos + far_halos + boxes + boxes2)
 
 
 def settle(adjoint, sens, adjoint_out, sens_out, sem):
@@ -550,7 +564,7 @@
                 vmem(18), vmem(2, 10), vmem(5, 4), vmem(3, 2 * n_cond), vmem(3, 2 * n_cond),
                 pltpu.SemaphoreType.DMA((6,)),
                 pltpu.SemaphoreType.DMA((64,)),
-                pltpu.SemaphoreType.DMA((29,)),
+                pltpu.SemaphoreType.DMA((30,)),
                 pltpu.SemaphoreType.DMA((6,)),
                 pltpu.SemaphoreType.REGULAR((2,)),
             ],

time: 35.9 us -> 35.1 us (0.978)
  Pallas kernels: 35.1 us -> 34.1 us
    pallas_call x1, Pallas kernels: 34.4 us -> 33.4 us  [local(): pl.pallas_call(functools.partial(kernel, n_cond, n_space), out_shape=(plt...]
where the time goes in v5:
time: 35.1 us; the launch traced here: 34.8 us
  Pallas kernels  34.1 us (97%)
  between operations  0.64 us (2%)
    pallas_call x1, Pallas kernels, local(): pl.pallas_call(functools.partial(kernel, n_cond, n_space), out_shape=(plt...  33.4 us

profile of v5, /device:TPU:32, one launch (start us, length us, event | category | flops | bytes accessed | tf_op | source)
XLA Modules:
  0.0 34.8 jit_solution(5668102968136487166)
XLA Ops:
  0.6 33.4 %shard_map.77 = (f32[2,5,4,8,128]{4,3,2,1,0:T(8,128)S(1)}, f32[4,2,128]{2,1,0:T(2,128)S(1)}) custom-call(f32[2,5,4,8,128]{4,3,2,1,0:T(8,128)} %target_in.1, f32[2,5,4,8,128]{4,3,2,1,0:T(8,128)} %shape_in.1, f32[3,5,2,5]{3,2,1,0:T(2,128)} %bitcast.1, f32[2,4,8,128]{3,2,1,0:T(8,128)} %sensor_in.1, f32[2]{0:T(128)} %shift_hbm.1, f32[2]{0:T(128)} %weight_hbm.1), custom_call_target="tpu_custom_call" | custom-call | tf_op jit(solution)/shard_map/pallas_call | solution.py:551
  34.1 0.7 %shard_map.78 = (f32[2,5,4,8,128]{4,3,2,1,0:T(8,128)}, f32[4,2,128]{2,1,0:T(2,128)}) custom-call(f32[2,5,4,8,128]{4,3,2,1,0:T(8,128)S(1)} %get-tuple-element.4.adjoint, f32[4,2,128]{2,1,0:T(2,128)S(1)} %get-tuple-element.5.sens), custom_call_target="tpu_custom_call" | custom-call | tf_op jit(solution)/shard_map/pallas_call | solution.py:575

commit v6 on v5

--- a/solution.py
+++ b/solution.py
@@ -139,7 +139,7 @@
 
 def kernel(
     n_cond, n_space, target_in, shape_in, jac_hbm, sensor_in, shift_hbm, weight_hbm, adjoint_out, sens_out,
-    jac_in, shift_in, weight_in, g, sen, shp, cpx, cyz, w, diag, jac, b0, b1, b2, halo, rs, rp1, rp2, sib, cs, rc, local_sem, send_sem, recv_sem, share_sem, known_sem,
+    jac_in, shift_in, weight_in, sen_stage, g_stage, g, sen, shp, cpx, cyz, w, diag, jac, b0, b1, b2, halo, rs, rp1, rp2, sib, cs, rc, local_sem, send_sem, recv_sem, share_sem, known_sem,
 ):
     space, cond = lax.axis_index("space"), lax.axis_index("cond")
     chip, core = space // 2, space % 2
@@ -183,18 +183,24 @@
         pltpu.make_async_copy(shift_hbm, shift_in, local_sem.at[4]),
         pltpu.make_async_copy(weight_hbm, weight_in, local_sem.at[5]),
     ]
-    for copy in small + mine:
+    stage = [
+        pltpu.make_async_copy(sensor_in, sen_stage, local_sem.at[6]),
+        pltpu.make_async_copy(target_in, g_stage, local_sem.at[7]),
+    ]
+    for copy in stage + small + mine:
         copy.start()
 
     pl.semaphore_wait(barrier, n_beside)
+    for copy in stage:
+        copy.wait()
 
     def to_right(k, j):
         low, size, at = ((2, 2, 0), (0, 4, 2))[k]
         s_low, s_size, s_at = ((1, 3, 0), (0, 4, 3))[k]
         there = 2 * (chip + 1) + j
         return [
-            remote(sensor_in.at[j, pl.ds(s_low, s_size)], sen.at[pl.ds(s_at, s_size)], 3 + 2 * k, there),
-            remote(target_in.at[j, :, pl.ds(low, size)], g.at[:, pl.ds(at, size)], 4 + 2 * k, there),
+            remote(sen_stage.at[j, pl.ds(s_low, s_size)], sen.at[pl.ds(s_at, s_size)], 3 + 2 * k, there),
+            remote(g_stage.at[j, :, pl.ds(low, size)], g.at[:, pl.ds(at, size)], 4 + 2 * k, there),
             remote(shape_in.at[j, :, pl.ds(low, size)], shp.at[:, pl.ds(at, size)], 21 + k, there),
         ]
 
@@ -203,8 +209,8 @@
         s_size, s_at = ((4, 15), (3, 19))[k]
         there = 2 * (chip - 1) + j
         return [
-            remote(sensor_in.at[j, pl.ds(0, s_size)], sen.at[pl.ds(s_at, s_size)], 7 + 2 * k, there),
-            remote(target_in.at[j, :, pl.ds(0, size)], g.at[:, pl.ds(at, size)], 8 + 2 * k, there),
+            remote(sen_stage.at[j, pl.ds(0, s_size)], sen.at[pl.ds(s_at, s_size)], 7 + 2 * k, there),
+            remote(g_stage.at[j, :, pl.ds(0, size)], g.at[:, pl.ds(at, size)], 8 + 2 * k, there),
             remote(shape_in.at[j, :, pl.ds(0, size)], shp.at[:, pl.ds(at, size)], 23 + k, there),
         ]
 
@@ -215,8 +221,8 @@
             first_round.append(([[c[i] for c in pairs] for i in range(3)], jnp.logical_and(there, core == k)))
     other = 1 - core
     swap = [
-        remote(sensor_in.at[other], sen.at[pl.ds(7 + 4 * core, 4)], 0, sibling),
-        remote(target_in.at[other], g.at[:, pl.ds(6 + 4 * core, 4)], 1, sibling),
+        remote(sen_stage.at[other], sen.at[pl.ds(7 + 4 * core, 4)], 0, sibling),
+        remote(g_stage.at[other], g.at[:, pl.ds(6 + 4 * core, 4)], 1, sibling),
         remote(shape_in.at[other], shp.at[:, pl.ds(6 + 4 * core, 4)], 2, sibling),
     ]
     def send_first(items):
@@ -507,6 +513,17 @@
             for i in range(4):
                 adjoint_out[c_at, v, i] = value[i] + fixes[v][i // 2]
 
+    over.wait_send()
+    boxes_over.wait_send()
+    for copy in swap:
+        copy.wait_send()
+    for copies, there in first_round:
+        @pl.when(there)
+        def _(copies=copies):
+            for copy in copies[0] + copies[1] + copies[2]:
+                copy.wait_send()
+    sent(early_halo + near_halos + far_halos + boxes + boxes2)
+
     for d, there in outer:
         pl.when(there)(shared(d, 2 * n_cond).wait_recv)
     shared(1, 2 * n_cond - 1).wait_recv()
@@ -516,19 +533,9 @@
             total = rc[d, i] if total is None else total + rc[d, i]
     for i in range(4):
         sens_out[i] = total[rows * i : rows * (i + 1)]
-    over.wait_send()
-    boxes_over.wait_send()
     for d, there in outer:
         pl.when(there)(shared(d, 2 * n_cond).wait_send)
     shared(1, 2 * n_cond - 1).wait_send()
-    for copy in swap:
-        copy.wait_send()
-    for copies, there in first_round:
-        @pl.when(there)
-        def _(copies=copies):
-            for copy in copies[0] + copies[1] + copies[2]:
-                copy.wait_send()
-    sent(early_halo + near_halos + far_halos + boxes + boxes2)
 
 
 def settle(adjoint, sens, adjoint_out, sens_out, sem):
@@ -558,11 +565,12 @@
             out_specs=(pl.BlockSpec(memory_space=pltpu.VMEM),) * 2,
             scratch_shapes=[
                 pltpu.SMEM((3, 5, 2, 5), F32), pltpu.SMEM((2,), F32), pltpu.SMEM((2,), F32),
+                vmem(2, 4), vmem(2, 5, 4),
                 vmem(5, 20), vmem(22), vmem(5, 20),
                 vmem(21), vmem(4, 20), vmem(20), vmem(20), vmem(75),
                 vmem(5, 24), vmem(5, 24), vmem(5, 24), vmem(5, 12), vmem(5, 4),
                 vmem(18), vmem(2, 10), vmem(5, 4), vmem(3, 2 * n_cond), vmem(3, 2 * n_cond),
-                pltpu.SemaphoreType.DMA((6,)),
+                pltpu.SemaphoreType.DMA((8,)),
                 pltpu.SemaphoreType.DMA((64,)),
                 pltpu.SemaphoreType.DMA((30,)),
                 pltpu.SemaphoreType.DMA((6,)),

time: 35.1 us -> 34.9 us (level)
  no operation moved by 1% of the time
where the time goes in v6:
time: 34.9 us; the launch traced here: 34.5 us
  Pallas kernels  33.9 us (97%)
  between operations  0.64 us (2%)
    pallas_call x1, Pallas kernels, local(): pl.pallas_call(functools.partial(kernel, n_cond, n_space), out_shape=(plt...  33.2 us

profile of v6, /device:TPU:32, one launch (start us, length us, event | category | flops | bytes accessed | tf_op | source)
XLA Modules:
  0.0 34.5 jit_solution(5004862691249191466)
XLA Ops:
  0.6 33.2 %shard_map.77 = (f32[2,5,4,8,128]{4,3,2,1,0:T(8,128)S(1)}, f32[4,2,128]{2,1,0:T(2,128)S(1)}) custom-call(f32[2,5,4,8,128]{4,3,2,1,0:T(8,128)} %target_in.1, f32[2,5,4,8,128]{4,3,2,1,0:T(8,128)} %shape_in.1, f32[3,5,2,5]{3,2,1,0:T(2,128)} %bitcast.1, f32[2,4,8,128]{3,2,1,0:T(8,128)} %sensor_in.1, f32[2]{0:T(128)} %shift_hbm.1, f32[2]{0:T(128)} %weight_hbm.1), custom_call_target="tpu_custom_call" | custom-call | tf_op jit(solution)/shard_map/pallas_call | solution.py:558
  33.8 0.7 %shard_map.78 = (f32[2,5,4,8,128]{4,3,2,1,0:T(8,128)}, f32[4,2,128]{2,1,0:T(2,128)}) custom-call(f32[2,5,4,8,128]{4,3,2,1,0:T(8,128)S(1)} %get-tuple-element.4.adjoint, f32[4,2,128]{2,1,0:T(2,128)S(1)} %get-tuple-element.5.sens), custom_call_target="tpu_custom_call" | custom-call | tf_op jit(solution)/shard_map/pallas_call | solution.py:583

commit v7 on v6

--- a/solution.py
+++ b/solution.py
@@ -458,8 +458,24 @@
             term = value * shp[v, i]
             total = term if total is None else total + term
         parts.append(weight * total)
+    me = 2 * cond + core
+
+    def share(d, j, c_to):
+        return pltpu.make_async_remote_copy(
+            src_ref=cs.at[d, j * n_cond + c_to], dst_ref=rc.at[2 - d, me], send_sem=share_sem.at[d], recv_sem=share_sem.at[5 - d],
+            device_id={"space": 2 * (chip + d - 1) + j, "cond": c_to},
+        )
+
+    def shared(d, slots):
+        return pltpu.make_async_remote_copy(
+            src_ref=cs.at[d, pl.ds(0, slots)], dst_ref=rc.at[d, pl.ds(0, slots)], send_sem=share_sem.at[d], recv_sem=share_sem.at[3 + d],
+            device_id={"space": sibling, "cond": cond},
+        )
+
+    pl.semaphore_wait(known_sem.at[1], 1)
     s2 = sublanes((8, 128))
-    for d in range(3):
+
+    def gather(d):
         for j in range(2):
             for c_to in range(n_cond):
                 gathered = jnp.zeros((8, 128), F32)
@@ -471,28 +487,17 @@
                         moved = parts[at] if turn == 0 else down(parts[at], turn)
                     gathered = jnp.where(s2 >= rows * i, moved, gathered) if i else moved
                 cs[d, j * n_cond + c_to] = gathered
-    me = 2 * cond + core
-
-    def share(d, j, c_to):
-        return pltpu.make_async_remote_copy(
-            src_ref=cs.at[d, j * n_cond + c_to], dst_ref=rc.at[2 - d, me], send_sem=share_sem.at[d], recv_sem=share_sem.at[5 - d],
-            device_id={"space": 2 * (chip + d - 1) + j, "cond": c_to},
-        )
-
-    def shared(d, slots):
-        return pltpu.make_async_remote_copy(
-            src_ref=cs.at[d, pl.ds(0, slots)], dst_ref=rc.at[d, pl.ds(0, slots)], send_sem=share_sem.at[d], recv_sem=share_sem.at[3 + d],
-            device_id={"space": sibling, "cond": cond},
-        )
-
-    pl.semaphore_wait(known_sem.at[1], 1)
+
     outer = ((0, has_left), (2, has_right))
+    gather(0)
+    gather(2)
     for dz in (2, 1, 3, 0):
         for d, there in outer:
             @pl.when(there)
             def _(d=d, dz=dz):
                 for j in range(2):
                     share(d, j, lax.rem(cond + dz, n_cond)).start()
+    gather(1)
     for s_to, c_to in reversed(ring[1:]):
         share(1, lax.rem(s_to, 2), c_to).start()
     rc[1, me] = cs[1, core * n_cond + cond]
@@ -524,13 +529,15 @@
                 copy.wait_send()
     sent(early_halo + near_halos + far_halos + boxes + boxes2)
 
+    def group(d):
+        pairs = [rc[d, i] + rc[d, i + n_cond] for i in range(n_cond)]
+        return sum(pairs[1:], pairs[0])
+
+    shared(1, 2 * n_cond - 1).wait_recv()
+    total = group(1)
     for d, there in outer:
         pl.when(there)(shared(d, 2 * n_cond).wait_recv)
-    shared(1, 2 * n_cond - 1).wait_recv()
-    total = None
-    for d in range(3):
-        for i in range(2 * n_cond):
-            total = rc[d, i] if total is None else total + rc[d, i]
+    total = total + (group(0) + group(2))
     for i in range(4):
         sens_out[i] = total[rows * i : rows * (i + 1)]
     for d, there in outer:

time: 34.9 us -> 34.9 us (level)
  no operation moved by 1% of the time
where the time goes in v7:
time: 34.9 us; the launch traced here: 34.5 us
  Pallas kernels  33.9 us (97%)
  between operations  0.64 us (2%)
    pallas_call x1, Pallas kernels, local(): pl.pallas_call(functools.partial(kernel, n_cond, n_space), out_shape=(plt...  33.2 us

profile of v7, /device:TPU:32, one launch (start us, length us, event | category | flops | bytes accessed | tf_op | source)
XLA Modules:
  0.0 34.5 jit_solution(8272768934190138567)
XLA Ops:
  0.6 33.2 %shard_map.77 = (f32[2,5,4,8,128]{4,3,2,1,0:T(8,128)S(1)}, f32[4,2,128]{2,1,0:T(2,128)S(1)}) custom-call(f32[2,5,4,8,128]{4,3,2,1,0:T(8,128)} %target_in.1, f32[2,5,4,8,128]{4,3,2,1,0:T(8,128)} %shape_in.1, f32[3,5,2,5]{3,2,1,0:T(2,128)} %bitcast.1, f32[2,4,8,128]{3,2,1,0:T(8,128)} %sensor_in.1, f32[2]{0:T(128)} %shift_hbm.1, f32[2]{0:T(128)} %weight_hbm.1), custom_call_target="tpu_custom_call" | custom-call | tf_op jit(solution)/shard_map/pallas_call | solution.py:565
  33.8 0.7 %shard_map.78 = (f32[2,5,4,8,128]{4,3,2,1,0:T(8,128)}, f32[4,2,128]{2,1,0:T(2,128)}) custom-call(f32[2,5,4,8,128]{4,3,2,1,0:T(8,128)S(1)} %get-tuple-element.4.adjoint, f32[4,2,128]{2,1,0:T(2,128)S(1)} %get-tuple-element.5.sens), custom_call_target="tpu_custom_call" | custom-call | tf_op jit(solution)/shard_map/pallas_call | solution.py:590
